TPU v7x, 256 devices: a whole 4x4x8 slice. The times are simulated.
256 devices in a mesh: ctx: 32 (over z, y), chan: 8 (over x, core).
Axes of the slice: x: 4, y: 4, z: 8, core: 2. Of those that a mesh axis runs over, the one named last changes fastest.
Arguments:
- query_slab: bfloat16 [7168, 1024], P('ctx', 'chan'), may hold values from -6 to 6
- key_slab: bfloat16 [7168, 1024], P('ctx', 'chan'), may hold values from -6 to 6
- value_slab: bfloat16 [7168, 1024], P('ctx', 'chan'), may hold values from -6 to 6
- filters: float32 [7168, 1024], P('ctx', 'chan'), may hold values from -1.1 to 1.1, as said below
- out_weight: bfloat16 [1024, 8192], P(None, 'chan'), may hold values from -0.1875 to 0.1875
- grad_out: bfloat16 [7168, 8192], P('ctx', 'chan'), may hold values from -5 to 5
Outputs:
- layer_out: float32 [7168, 8192], P('ctx', 'chan')
- grad_query: float32 [7168, 1024], P('ctx', 'chan')
- grad_key: float32 [7168, 1024], P('ctx', 'chan')
- grad_value: float32 [7168, 1024], P('ctx', 'chan')
- grad_weight: float32 [1024, 8192], P('ctx', 'chan')
Inputs may be any that keep to these rules, and one draw needn't show every extreme that they name: Real causal filters, one per channel.
All inputs are finite; a program needn't handle non-finite values.
Results may differ from a plain program's by a relative error of at most 0.0029.
Values may be sent and summed in bfloat16 or wider, within the bound.
No kernel may reach another device: no remote copies, remote signals or barrier semaphores. Data moves between devices by JAX's collectives and lax.ppermute only.
A program may use at most 64 MiB of HBM per device.

v0:
```python
import math

import jax
import jax.numpy as jnp
from jax import lax
from jax.sharding import PartitionSpec as P

HIGHEST = lax.Precision.HIGHEST


def swapped(block, axis, bit):
    count = lax.axis_size(axis)
    route = []
    for low in range(count):
        high = low | 1 << bit
        if high != low and high < count:
            route += [(low, high), (high, low)]
    return lax.ppermute(block, axis, route)


def phase_pair(numer, denom):
    angle_rad = -2.0 * math.pi / denom * numer.astype(jnp.float32)
    return (jnp.cos(angle_rad), jnp.sin(angle_rad))


def complex_mul(left_factor, right_factor):
    real_part = left_factor[0] * right_factor[0] - left_factor[1] * right_factor[1]
    imag_part = left_factor[0] * right_factor[1] + left_factor[1] * right_factor[0]
    return jnp.stack([real_part, imag_part])


def complex_table(table_cos, table_sin, operand, form):

    def apply_table(table, values):
        return jnp.einsum(form, table, values, precision=HIGHEST)

    real_part = apply_table(table_cos, operand[0]) - apply_table(table_sin, operand[1])
    imag_part = apply_table(table_cos, operand[1]) + apply_table(table_sin, operand[0])
    return jnp.stack([real_part, imag_part])


def local_transform(spectrum, adjoint):
    tok_rows = spectrum.shape[3]
    grid = lax.broadcasted_iota(jnp.int32, (tok_rows, tok_rows), 0) * lax.broadcasted_iota(
        jnp.int32, (tok_rows, tok_rows), 1
    )
    table_cos, table_sin = phase_pair(grid % tok_rows, tok_rows)
    if adjoint:
        return complex_table(table_cos / tok_rows, -table_sin / tok_rows, spectrum, "kn,aenc->aekc")
    return complex_table(table_cos, table_sin, spectrum, "kn,aenc->aekc")


def row_twiddle(freq_row, tok_rows, padded_len, adjoint):
    positions = lax.broadcasted_iota(jnp.int32, (2, tok_rows, 1), 1)
    parity = lax.broadcasted_iota(jnp.int32, (2, tok_rows, 1), 0)
    turn_cos, turn_sin = phase_pair(positions * (2 * freq_row + parity) % padded_len, padded_len)
    if adjoint:
        turn_sin = -turn_sin
    return jnp.stack([turn_cos, turn_sin])[:, None]


def butterfly_forward(spectrum, group_size, own_index):
    section_count = group_size.bit_length() - 1
    for bit_num in reversed(range(section_count)):
        half_span = 1 << bit_num
        partner_block = swapped(spectrum, "ctx", bit_num)
        upper_half = own_index >> bit_num & 1 == 1
        turn_cos, turn_sin = phase_pair(own_index % half_span, 2 * half_span)
        low_value = spectrum + partner_block
        high_value = complex_mul(partner_block - spectrum, jnp.stack([turn_cos, turn_sin]))
        spectrum = jnp.where(upper_half, high_value, low_value)
    return spectrum


def butterfly_inverse(spectrum, group_size, own_index):
    section_count = group_size.bit_length() - 1
    for bit_num in range(section_count):
        half_span = 1 << bit_num
        partner_block = swapped(spectrum, "ctx", bit_num)
        upper_half = own_index >> bit_num & 1 == 1
        turn_cos, turn_sin = phase_pair(own_index % half_span, 2 * half_span)
        conj_turn = jnp.stack([turn_cos, -turn_sin])
        low_value = 0.5 * (spectrum + complex_mul(partner_block, conj_turn))
        high_value = 0.5 * (partner_block - complex_mul(spectrum, conj_turn))
        spectrum = jnp.where(upper_half, high_value, low_value)
    return spectrum


def reversed_row(own_index, group_size):
    section_count = group_size.bit_length() - 1
    result_row = own_index * 0
    for bit_num in range(section_count):
        result_row = result_row + ((own_index >> bit_num & 1) << section_count - 1 - bit_num)
    return result_row


def frequency_row(own_index, group_size):
    return reversed_row(own_index, group_size)


def across_context(spectrum, group_size, own_index, adjoint):
    if adjoint:
        moved = butterfly_inverse(spectrum, group_size, own_index)
    else:
        moved = butterfly_forward(spectrum, group_size, own_index)
    return moved


def to_frequency(signal, imag_signal, group_size, own_index):
    tok_rows = signal.shape[1]
    padded_len = 2 * group_size * tok_rows
    turn_cos, turn_sin = phase_pair(own_index, 2 * group_size)
    real_part = jnp.stack([signal, signal * turn_cos - imag_signal * turn_sin], axis=1)
    imag_part = jnp.stack([imag_signal, signal * turn_sin + imag_signal * turn_cos], axis=1)
    spectrum = across_context(jnp.stack([real_part, imag_part]), group_size, own_index, False)
    turned = complex_mul(
        spectrum, row_twiddle(frequency_row(own_index, group_size), tok_rows, padded_len, False)
    )
    return local_transform(turned, False)


def from_frequency(spectrum, group_size, own_index):
    tok_rows = spectrum.shape[3]
    padded_len = 2 * group_size * tok_rows
    back = local_transform(spectrum, True)
    turned = complex_mul(
        back, row_twiddle(frequency_row(own_index, group_size), tok_rows, padded_len, True)
    )
    moved = across_context(turned, group_size, own_index, True)
    turn_cos, turn_sin = phase_pair(own_index, 2 * group_size)
    real_out = 0.5 * (moved[0][:, 0] + moved[0][:, 1] * turn_cos + moved[1][:, 1] * turn_sin)
    imag_out = 0.5 * (moved[1][:, 0] + moved[1][:, 1] * turn_cos - moved[0][:, 1] * turn_sin)
    return (real_out, imag_out)


def local(query_slab, key_slab, value_slab, filters, out_weight, grad_out):
    group_size = lax.axis_size("ctx")
    own_index = lax.axis_index("ctx")
    query_f = query_slab.astype(jnp.float32)
    key_f = key_slab.astype(jnp.float32)
    value_f = value_slab.astype(jnp.float32)
    mixed_input = key_f * value_f
    conj_sign = jnp.array([1.0, -1.0], jnp.float32).reshape(2, 1, 1, 1)
    partial_terms = lax.dot_general(
        grad_out, out_weight, (((1,), (1,)), ((), ())), preferred_element_type=jnp.float32
    )
    grad_gated = lax.psum_scatter(partial_terms, "chan", scatter_dimension=1, tiled=True)
    grad_conv = grad_gated * query_f
    spectra = to_frequency(
        jnp.stack([mixed_input, filters]),
        jnp.zeros((2,) + filters.shape, jnp.float32),
        group_size,
        own_index,
    )
    signal_spec = spectra[:, 0]
    filter_spec = spectra[:, 1]
    conv_out = from_frequency(
        complex_mul(signal_spec, filter_spec)[:, None], group_size, own_index
    )[0][0]
    grad_spec = to_frequency(
        grad_conv[None], jnp.zeros_like(grad_conv)[None], group_size, own_index
    )[:, 0]
    grad_mixed = from_frequency(
        complex_mul(grad_spec, filter_spec * conj_sign)[:, None], group_size, own_index
    )[0][0]
    gated_out = (query_f * conv_out).astype(jnp.bfloat16)
    full_gated = lax.all_gather(gated_out, "chan", axis=1, tiled=True)
    layer_out = jnp.dot(full_gated, out_weight, preferred_element_type=jnp.float32)
    grad_query = grad_gated * conv_out
    grad_key = grad_mixed * value_f
    grad_value = grad_mixed * key_f
    grad_weight = lax.psum_scatter(
        lax.dot_general(
            full_gated, grad_out, (((0,), (0,)), ((), ())), preferred_element_type=jnp.float32
        ),
        "ctx",
        scatter_dimension=0,
        tiled=True,
    )
    return (layer_out, grad_query, grad_key, grad_value, grad_weight)


def solution(mesh):
    placed = (
        P("ctx", "chan"),
        P("ctx", "chan"),
        P("ctx", "chan"),
        P("ctx", "chan"),
        P(None, "chan"),
        P("ctx", "chan"),
    )
    return jax.shard_map(
        local,
        mesh=mesh,
        in_specs=placed,
        out_specs=(
            P("ctx", "chan"),
            P("ctx", "chan"),
            P("ctx", "chan"),
            P("ctx", "chan"),
            P("ctx", "chan"),
        ),
        check_vma=False,
    )
```

profile of v0, /device:TPU:1, one launch (start us, length us, event | category | flops | bytes accessed | tf_op | source)
XLA Modules:
  0.0 597.5 jit_solution(11677567668699667229)
XLA Ops:
  11.3 7.7 %collective-permute-start = (f32[2,2,2,224,128]{4,3,2,1,0:T(8,128)}, f32[2,2,2,224,128]{4,3,2,1,0:T(8,128)}, u32[]{:S(2)}, u32[]{:S(2)}) collective-permute-start(f32[2,2,2,224,128]{4,3,2,1,0:T(8,128)} %pad_maximum_fusion), channel_id=1, source_target_pairs={{0,128},{128,0},{8,136},{136,8},{16,144},{144,16},{24,152},{152,24... | collective-permute-start | bytes 2752520 | tf_op jit(solution)/shard_map/ppermute | solution.py:18
  19.2 24.3 %collective-permute-done = f32[2,2,2,224,128]{4,3,2,1,0:T(8,128)} collective-permute-done((f32[2,2,2,224,128]{4,3,2,1,0:T(8,128)}, f32[2,2,2,224,128]{4,3,2,1,0:T(8,128)}, u32[]{:S(2)}, u32[]{:S(2)}) %collective-permute-start) | collective-permute-done | bytes 917536 | tf_op jit(solution)/shard_map/ppermute | solution.py:18
  47.9 17.1 %collective-permute-start.1 = (f32[2,2,2,224,128]{4,3,2,1,0:T(8,128)}, f32[2,2,2,224,128]{4,3,2,1,0:T(8,128)}, u32[]{:S(2)}, u32[]{:S(2)}) collective-permute-start(f32[2,2,2,224,128]{4,3,2,1,0:T(8,128)} %maximum_select_fusion), channel_id=1, source_target_pairs={{0,64},{64,0},{8,72},{72,8},{16,80},{80,16},{24,88},{88,24},{32,96... | collective-permute-start | bytes 2752520 | tf_op jit(solution)/shard_map/ppermute | solution.py:18
  65.2 39.3 %collective-permute-done.1 = f32[2,2,2,224,128]{4,3,2,1,0:T(8,128)} collective-permute-done((f32[2,2,2,224,128]{4,3,2,1,0:T(8,128)}, f32[2,2,2,224,128]{4,3,2,1,0:T(8,128)}, u32[]{:S(2)}, u32[]{:S(2)}) %collective-permute-start.1) | collective-permute-done | bytes 917536 | tf_op jit(solution)/shard_map/ppermute | solution.py:18
  109.2 20.0 %collective-permute-done.2 = f32[2,2,2,224,128]{4,3,2,1,0:T(8,128)S(1)} collective-permute-done((f32[2,2,2,224,128]{4,3,2,1,0:T(8,128)}, f32[2,2,2,224,128]{4,3,2,1,0:T(8,128)S(1)}, u32[]{:S(2)}, u32[]{:S(2)}) %collective-permute-start.2) | collective-permute-done | bytes 917536 | tf_op jit(solution)/shard_map/ppermute | solution.py:18
  135.8 17.6 %collective-permute-done.3 = f32[2,2,2,224,128]{4,3,2,1,0:T(8,128)} collective-permute-done((f32[2,2,2,224,128]{4,3,2,1,0:T(8,128)S(1)}, f32[2,2,2,224,128]{4,3,2,1,0:T(8,128)}, u32[]{:S(2)}, u32[]{:S(2)}) %collective-permute-start.3) | collective-permute-done | bytes 917536 | tf_op jit(solution)/shard_map/ppermute | solution.py:18
  158.2 16.8 %collective-permute-done.4 = f32[2,2,2,224,128]{4,3,2,1,0:T(8,128)} collective-permute-done((f32[2,2,2,224,128]{4,3,2,1,0:T(8,128)S(1)}, f32[2,2,2,224,128]{4,3,2,1,0:T(8,128)}, u32[]{:S(2)}, u32[]{:S(2)}) %collective-permute-start.4) | collective-permute-done | bytes 917536 | tf_op jit(solution)/shard_map/ppermute | solution.py:18
  191.9 6.0 %collective-permute-done.5 = f32[2,1,2,224,128]{4,3,2,1,0:T(8,128)S(1)} collective-permute-done((f32[2,1,2,224,128]{4,3,2,1,0:T(8,128)S(1)}, f32[2,1,2,224,128]{4,3,2,1,0:T(8,128)S(1)}, u32[]{:S(2)}, u32[]{:S(2)}) %collective-permute-start.5) | collective-permute-done | bytes 458784 | tf_op jit(solution)/shard_map/ppermute | solution.py:18
  201.9 9.2 %collective-permute-done.6 = f32[2,1,2,224,128]{4,3,2,1,0:T(8,128)} collective-permute-done((f32[2,1,2,224,128]{4,3,2,1,0:T(8,128)S(1)}, f32[2,1,2,224,128]{4,3,2,1,0:T(8,128)}, u32[]{:S(2)}, u32[]{:S(2)}) %collective-permute-start.6) | collective-permute-done | bytes 458784 | tf_op jit(solution)/shard_map/ppermute | solution.py:18
  215.1 6.1 %collective-permute-done.7 = f32[2,1,2,224,128]{4,3,2,1,0:T(8,128)S(1)} collective-permute-done((f32[2,1,2,224,128]{4,3,2,1,0:T(8,128)S(1)}, f32[2,1,2,224,128]{4,3,2,1,0:T(8,128)S(1)}, u32[]{:S(2)}, u32[]{:S(2)}) %collective-permute-start.7) | collective-permute-done | bytes 458784 | tf_op jit(solution)/shard_map/ppermute | solution.py:18
  223.0 13.7 %collective-permute-start.8 = (f32[2,1,2,224,128]{4,3,2,1,0:T(8,128)S(1)}, f32[2,1,2,224,128]{4,3,2,1,0:T(8,128)S(1)}, u32[]{:S(2)}, u32[]{:S(2)}) collective-permute-start(f32[2,1,2,224,128]{4,3,2,1,0:T(8,128)S(1)} %fusion.17), channel_id=1, source_target_pairs={{0,64},{64,0},{8,72},{72,8},{16,80},{80,16},{24,88},{88,24},{32,96... | collective-permute-start | bytes 1376264 | tf_op jit(solution)/shard_map/ppermute | solution.py:18
  238.6 19.5 %collective-permute-done.8 = f32[2,1,2,224,128]{4,3,2,1,0:T(8,128)S(1)} collective-permute-done((f32[2,1,2,224,128]{4,3,2,1,0:T(8,128)S(1)}, f32[2,1,2,224,128]{4,3,2,1,0:T(8,128)S(1)}, u32[]{:S(2)}, u32[]{:S(2)}) %collective-permute-start.8) | collective-permute-done | bytes 458784 | tf_op jit(solution)/shard_map/ppermute | solution.py:18
  260.5 22.8 %collective-permute-done.9 = f32[2,1,2,224,128]{4,3,2,1,0:T(8,128)S(1)} collective-permute-done((f32[2,1,2,224,128]{4,3,2,1,0:T(8,128)S(1)}, f32[2,1,2,224,128]{4,3,2,1,0:T(8,128)S(1)}, u32[]{:S(2)}, u32[]{:S(2)}) %collective-permute-start.9) | collective-permute-done | bytes 458784 | tf_op jit(solution)/shard_map/ppermute | solution.py:18
  288.4 21.3 %collective-permute-done.10 = f32[2,1,2,224,128]{4,3,2,1,0:T(8,128)S(1)} collective-permute-done((f32[2,1,2,224,128]{4,3,2,1,0:T(8,128)S(1)}, f32[2,1,2,224,128]{4,3,2,1,0:T(8,128)S(1)}, u32[]{:S(2)}, u32[]{:S(2)}) %collective-permute-start.10) | collective-permute-done | bytes 458784 | tf_op jit(solution)/shard_map/ppermute | solution.py:18
  310.0 22.8 %collective-permute-done.11 = f32[2,1,2,224,128]{4,3,2,1,0:T(8,128)S(1)} collective-permute-done((f32[2,1,2,224,128]{4,3,2,1,0:T(8,128)S(1)}, f32[2,1,2,224,128]{4,3,2,1,0:T(8,128)S(1)}, u32[]{:S(2)}, u32[]{:S(2)}) %collective-permute-start.11) | collective-permute-done | bytes 458784 | tf_op jit(solution)/shard_map/ppermute | solution.py:18
  333.2 11.6 %collective-permute-done.12 = f32[2,1,2,224,128]{4,3,2,1,0:T(8,128)S(1)} collective-permute-done((f32[2,1,2,224,128]{4,3,2,1,0:T(8,128)S(1)}, f32[2,1,2,224,128]{4,3,2,1,0:T(8,128)S(1)}, u32[]{:S(2)}, u32[]{:S(2)}) %collective-permute-start.12) | collective-permute-done | bytes 458784 | tf_op jit(solution)/shard_map/ppermute | solution.py:18
  345.1 13.8 %all_gather.3 = bf16[224,1024]{1,0:T(8,128)(2,1)S(1)} all-gather(bf16[224,128]{1,0:T(8,128)(2,1)S(1)} %fusion.98), channel_id=1, replica_groups=mesh['ctx'=32,'chan'=8] {'chan'}, dimensions={1}, use_global_device_ids=true | all-gather | bytes 516096 | tf_op jit(solution)/shard_map/all_gather | solution.py:167
  363.9 7.7 %collective-permute-done.14 = f32[2,1,2,224,128]{4,3,2,1,0:T(8,128)} collective-permute-done((f32[2,1,2,224,128]{4,3,2,1,0:T(8,128)}, f32[2,1,2,224,128]{4,3,2,1,0:T(8,128)}, u32[]{:S(2)}, u32[]{:S(2)}) %collective-permute-start.14) | collective-permute-done | bytes 458784 | tf_op jit(solution)/shard_map/ppermute | solution.py:18
  386.3 10.6 %collective-permute-done.15 = f32[2,1,2,224,128]{4,3,2,1,0:T(8,128)S(1)} collective-permute-done((f32[2,1,2,224,128]{4,3,2,1,0:T(8,128)S(1)}, f32[2,1,2,224,128]{4,3,2,1,0:T(8,128)S(1)}, u32[]{:S(2)}, u32[]{:S(2)}) %collective-permute-start.15) | collective-permute-done | bytes 458784 | tf_op jit(solution)/shard_map/ppermute | solution.py:18
  401.4 10.1 %collective-permute-done.16 = f32[2,1,2,224,128]{4,3,2,1,0:T(8,128)S(1)} collective-permute-done((f32[2,1,2,224,128]{4,3,2,1,0:T(8,128)S(1)}, f32[2,1,2,224,128]{4,3,2,1,0:T(8,128)S(1)}, u32[]{:S(2)}, u32[]{:S(2)}) %collective-permute-start.16) | collective-permute-done | bytes 458784 | tf_op jit(solution)/shard_map/ppermute | solution.py:18
  412.0 11.8 %collective-permute-done.17 = f32[2,1,2,224,128]{4,3,2,1,0:T(8,128)S(1)} collective-permute-done((f32[2,1,2,224,128]{4,3,2,1,0:T(8,128)S(1)}, f32[2,1,2,224,128]{4,3,2,1,0:T(8,128)S(1)}, u32[]{:S(2)}, u32[]{:S(2)}) %collective-permute-start.17) | collective-permute-done | bytes 458784 | tf_op jit(solution)/shard_map/ppermute | solution.py:18
  425.4 24.9 %collective-permute-done.18 = f32[2,1,2,224,128]{4,3,2,1,0:T(8,128)S(1)} collective-permute-done((f32[2,1,2,224,128]{4,3,2,1,0:T(8,128)S(1)}, f32[2,1,2,224,128]{4,3,2,1,0:T(8,128)S(1)}, u32[]{:S(2)}, u32[]{:S(2)}) %collective-permute-start.18) | collective-permute-done | bytes 458784 | tf_op jit(solution)/shard_map/ppermute | solution.py:18
  454.5 24.4 %collective-permute-done.19 = f32[2,1,2,224,128]{4,3,2,1,0:T(8,128)S(1)} collective-permute-done((f32[2,1,2,224,128]{4,3,2,1,0:T(8,128)S(1)}, f32[2,1,2,224,128]{4,3,2,1,0:T(8,128)S(1)}, u32[]{:S(2)}, u32[]{:S(2)}) %collective-permute-start.19) | collective-permute-done | bytes 458784 | tf_op jit(solution)/shard_map/ppermute | solution.py:18
  480.5 110.0 %reduce-scatter.5.cloned.1.call-done = f32[32,1024]{1,0:T(8,128)} async-done(((f32[1024,1024]{1,0:T(8,128)}), f32[32,1024]{1,0:T(8,128)}) %reduce-scatter.5.cloned.1.call-update) | async-done | bytes 131088 | tf_op jit(solution)/shard_map/reduce_scatter | solution.py:172
  (162 shorter events, 92.6 us)
Async XLA Ops:
  7.2 229.6 %copy-start = (bf16[1024,1024]{1,0:T(8,128)(2,1)S(1)}, bf16[1024,1024]{1,0:T(8,128)(2,1)}, u32[]{:S(2)}) copy-start(bf16[1024,1024]{1,0:T(8,128)(2,1)} %param.11) | copy-start | bytes 6291460
  7.2 276.3 %reduce-scatter.3.cloned.1.call-start = ((), (), s32[]{:S(2)}) async-start(), calls=%async_computation.2 | async-start | bytes 1032192 | tf_op jit(solution)/shard_map/reduce_scatter | solution.py:147
  11.3 32.2 %collective-permute-start = (f32[2,2,2,224,128]{4,3,2,1,0:T(8,128)}, f32[2,2,2,224,128]{4,3,2,1,0:T(8,128)}, u32[]{:S(2)}, u32[]{:S(2)}) collective-permute-start(f32[2,2,2,224,128]{4,3,2,1,0:T(8,128)} %pad_maximum_fusion), channel_id=1, source_target_pairs={{0,128},{128,0},{8,136},{136,8},{16,144},{144,16},{24,152},{152,24... | collective-permute-start | bytes 2752520 | tf_op jit(solution)/shard_map/ppermute | solution.py:18
  47.9 56.6 %collective-permute-start.1 = (f32[2,2,2,224,128]{4,3,2,1,0:T(8,128)}, f32[2,2,2,224,128]{4,3,2,1,0:T(8,128)}, u32[]{:S(2)}, u32[]{:S(2)}) collective-permute-start(f32[2,2,2,224,128]{4,3,2,1,0:T(8,128)} %maximum_select_fusion), channel_id=1, source_target_pairs={{0,64},{64,0},{8,72},{72,8},{16,80},{80,16},{24,88},{88,24},{32,96... | collective-permute-start | bytes 2752520 | tf_op jit(solution)/shard_map/ppermute | solution.py:18
  65.2 41.1 %copy-start.3 = (f32[1,2,2,224,128]{4,3,2,1,0:T(8,128)S(1)}, f32[1,2,2,224,128]{4,3,2,1,0:T(8,128)}, u32[]{:S(2)}) copy-start(f32[1,2,2,224,128]{4,3,2,1,0:T(8,128)} %copy-done.2) | copy-start | bytes 1376260
  109.0 20.2 %collective-permute-start.2 = (f32[2,2,2,224,128]{4,3,2,1,0:T(8,128)}, f32[2,2,2,224,128]{4,3,2,1,0:T(8,128)S(1)}, u32[]{:S(2)}, u32[]{:S(2)}) collective-permute-start(f32[2,2,2,224,128]{4,3,2,1,0:T(8,128)} %maximum_select_fusion.1), channel_id=1, source_target_pairs={{0,32},{32,0},{8,40},{40,8},{16,48},{48,16},{24,56},{56,24},{64,96... | collective-permute-start | bytes 2752520 | tf_op jit(solution)/shard_map/ppermute | solution.py:18
  132.6 20.8 %collective-permute-start.3 = (f32[2,2,2,224,128]{4,3,2,1,0:T(8,128)S(1)}, f32[2,2,2,224,128]{4,3,2,1,0:T(8,128)}, u32[]{:S(2)}, u32[]{:S(2)}) collective-permute-start(f32[2,2,2,224,128]{4,3,2,1,0:T(8,128)S(1)} %maximum_select_fusion.2), channel_id=1, source_target_pairs={{0,16},{16,0},{8,24},{24,8},{32,48},{48,32},{40,56},{56,40},{64,80... | collective-permute-start | bytes 2752520 | tf_op jit(solution)/shard_map/ppermute | solution.py:18
  156.4 18.6 %collective-permute-start.4 = (f32[2,2,2,224,128]{4,3,2,1,0:T(8,128)S(1)}, f32[2,2,2,224,128]{4,3,2,1,0:T(8,128)}, u32[]{:S(2)}, u32[]{:S(2)}) collective-permute-start(f32[2,2,2,224,128]{4,3,2,1,0:T(8,128)S(1)} %maximum_select_fusion.3), channel_id=1, source_target_pairs={{0,8},{8,0},{16,24},{24,16},{32,40},{40,32},{48,56},{56,48},{64,72... | collective-permute-start | bytes 2752520 | tf_op jit(solution)/shard_map/ppermute | solution.py:18
  190.5 7.4 %collective-permute-start.5 = (f32[2,1,2,224,128]{4,3,2,1,0:T(8,128)S(1)}, f32[2,1,2,224,128]{4,3,2,1,0:T(8,128)S(1)}, u32[]{:S(2)}, u32[]{:S(2)}) collective-permute-start(f32[2,1,2,224,128]{4,3,2,1,0:T(8,128)S(1)} %pad_maximum_fusion.2), channel_id=1, source_target_pairs={{0,8},{8,0},{16,24},{24,16},{32,40},{40,32},{48,56},{56,48},{64,72... | collective-permute-start | bytes 1376264 | tf_op jit(solution)/shard_map/ppermute | solution.py:18
  198.8 12.2 %collective-permute-start.6 = (f32[2,1,2,224,128]{4,3,2,1,0:T(8,128)S(1)}, f32[2,1,2,224,128]{4,3,2,1,0:T(8,128)}, u32[]{:S(2)}, u32[]{:S(2)}) collective-permute-start(f32[2,1,2,224,128]{4,3,2,1,0:T(8,128)S(1)} %fusion.11), channel_id=1, source_target_pairs={{0,16},{16,0},{8,24},{24,8},{32,48},{48,32},{40,56},{56,40},{64,80... | collective-permute-start | bytes 1376264 | tf_op jit(solution)/shard_map/ppermute | solution.py:18
  213.7 7.4 %collective-permute-start.7 = (f32[2,1,2,224,128]{4,3,2,1,0:T(8,128)S(1)}, f32[2,1,2,224,128]{4,3,2,1,0:T(8,128)S(1)}, u32[]{:S(2)}, u32[]{:S(2)}) collective-permute-start(f32[2,1,2,224,128]{4,3,2,1,0:T(8,128)S(1)} %fusion.14), channel_id=1, source_target_pairs={{0,32},{32,0},{8,40},{40,8},{16,48},{48,16},{24,56},{56,24},{64,96... | collective-permute-start | bytes 1376264 | tf_op jit(solution)/shard_map/ppermute | solution.py:18
  223.0 35.1 %collective-permute-start.8 = (f32[2,1,2,224,128]{4,3,2,1,0:T(8,128)S(1)}, f32[2,1,2,224,128]{4,3,2,1,0:T(8,128)S(1)}, u32[]{:S(2)}, u32[]{:S(2)}) collective-permute-start(f32[2,1,2,224,128]{4,3,2,1,0:T(8,128)S(1)} %fusion.17), channel_id=1, source_target_pairs={{0,64},{64,0},{8,72},{72,8},{16,80},{80,16},{24,88},{88,24},{32,96... | collective-permute-start | bytes 1376264 | tf_op jit(solution)/shard_map/ppermute | solution.py:18
  238.5 352.0 %reduce-scatter.5.cloned.1.call-start = ((), (), s32[]{:S(2)}) async-start(), calls=%async_computation.3 | async-start | bytes 4325376 | tf_op jit(solution)/shard_map/reduce_scatter | solution.py:172
  258.3 25.0 %collective-permute-start.9 = (f32[2,1,2,224,128]{4,3,2,1,0:T(8,128)S(1)}, f32[2,1,2,224,128]{4,3,2,1,0:T(8,128)S(1)}, u32[]{:S(2)}, u32[]{:S(2)}) collective-permute-start(f32[2,1,2,224,128]{4,3,2,1,0:T(8,128)S(1)} %fusion.20), channel_id=1, source_target_pairs={{0,128},{128,0},{8,136},{136,8},{16,144},{144,16},{24,152},{152,24... | collective-permute-start | bytes 1376264 | tf_op jit(solution)/shard_map/ppermute | solution.py:18
  285.2 24.5 %collective-permute-start.10 = (f32[2,1,2,224,128]{4,3,2,1,0:T(8,128)S(1)}, f32[2,1,2,224,128]{4,3,2,1,0:T(8,128)S(1)}, u32[]{:S(2)}, u32[]{:S(2)}) collective-permute-start(f32[2,1,2,224,128]{4,3,2,1,0:T(8,128)S(1)} %pad_maximum_fusion.3), channel_id=1, source_target_pairs={{0,128},{128,0},{8,136},{136,8},{16,144},{144,16},{24,152},{152,24... | collective-permute-start | bytes 1376264 | tf_op jit(solution)/shard_map/ppermute | solution.py:18
  309.9 22.9 %collective-permute-start.11 = (f32[2,1,2,224,128]{4,3,2,1,0:T(8,128)S(1)}, f32[2,1,2,224,128]{4,3,2,1,0:T(8,128)S(1)}, u32[]{:S(2)}, u32[]{:S(2)}) collective-permute-start(f32[2,1,2,224,128]{4,3,2,1,0:T(8,128)S(1)} %maximum_select_fusion.5), channel_id=1, source_target_pairs={{0,64},{64,0},{8,72},{72,8},{16,80},{80,16},{24,88},{88,24},{32,96... | collective-permute-start | bytes 1376264 | tf_op jit(solution)/shard_map/ppermute | solution.py:18
  333.1 11.7 %collective-permute-start.12 = (f32[2,1,2,224,128]{4,3,2,1,0:T(8,128)S(1)}, f32[2,1,2,224,128]{4,3,2,1,0:T(8,128)S(1)}, u32[]{:S(2)}, u32[]{:S(2)}) collective-permute-start(f32[2,1,2,224,128]{4,3,2,1,0:T(8,128)S(1)} %maximum_select_fusion.6), channel_id=1, source_target_pairs={{0,32},{32,0},{8,40},{40,8},{16,48},{48,16},{24,56},{56,24},{64,96... | collective-permute-start | bytes 1376264 | tf_op jit(solution)/shard_map/ppermute | solution.py:18
  344.9 13.9 %collective-permute-start.13 = (f32[2,1,2,224,128]{4,3,2,1,0:T(8,128)S(1)}, f32[2,1,2,224,128]{4,3,2,1,0:T(8,128)S(1)}, u32[]{:S(2)}, u32[]{:S(2)}) collective-permute-start(f32[2,1,2,224,128]{4,3,2,1,0:T(8,128)S(1)} %maximum_select_fusion.7), channel_id=1, source_target_pairs={{0,16},{16,0},{8,24},{24,8},{32,48},{48,32},{40,56},{56,40},{64,80... | collective-permute-start | bytes 1376264 | tf_op jit(solution)/shard_map/ppermute | solution.py:18
  359.8 11.8 %collective-permute-start.14 = (f32[2,1,2,224,128]{4,3,2,1,0:T(8,128)}, f32[2,1,2,224,128]{4,3,2,1,0:T(8,128)}, u32[]{:S(2)}, u32[]{:S(2)}) collective-permute-start(f32[2,1,2,224,128]{4,3,2,1,0:T(8,128)} %maximum_select_fusion.8), channel_id=1, source_target_pairs={{0,8},{8,0},{16,24},{24,16},{32,40},{40,32},{48,56},{56,48},{64,72... | collective-permute-start | bytes 1376264 | tf_op jit(solution)/shard_map/ppermute | solution.py:18
  385.8 11.0 %collective-permute-start.15 = (f32[2,1,2,224,128]{4,3,2,1,0:T(8,128)S(1)}, f32[2,1,2,224,128]{4,3,2,1,0:T(8,128)S(1)}, u32[]{:S(2)}, u32[]{:S(2)}) collective-permute-start(f32[2,1,2,224,128]{4,3,2,1,0:T(8,128)S(1)} %pad_maximum_fusion.4), channel_id=1, source_target_pairs={{0,8},{8,0},{16,24},{24,16},{32,40},{40,32},{48,56},{56,48},{64,72... | collective-permute-start | bytes 1376264 | tf_op jit(solution)/shard_map/ppermute | solution.py:18
  397.0 14.5 %collective-permute-start.16 = (f32[2,1,2,224,128]{4,3,2,1,0:T(8,128)S(1)}, f32[2,1,2,224,128]{4,3,2,1,0:T(8,128)S(1)}, u32[]{:S(2)}, u32[]{:S(2)}) collective-permute-start(f32[2,1,2,224,128]{4,3,2,1,0:T(8,128)S(1)} %fusion.26), channel_id=1, source_target_pairs={{0,16},{16,0},{8,24},{24,8},{32,48},{48,32},{40,56},{56,40},{64,80... | collective-permute-start | bytes 1376264 | tf_op jit(solution)/shard_map/ppermute | solution.py:18
  411.8 12.1 %collective-permute-start.17 = (f32[2,1,2,224,128]{4,3,2,1,0:T(8,128)S(1)}, f32[2,1,2,224,128]{4,3,2,1,0:T(8,128)S(1)}, u32[]{:S(2)}, u32[]{:S(2)}) collective-permute-start(f32[2,1,2,224,128]{4,3,2,1,0:T(8,128)S(1)} %fusion.29), channel_id=1, source_target_pairs={{0,32},{32,0},{8,40},{40,8},{16,48},{48,16},{24,56},{56,24},{64,96... | collective-permute-start | bytes 1376264 | tf_op jit(solution)/shard_map/ppermute | solution.py:18
  424.0 26.3 %collective-permute-start.18 = (f32[2,1,2,224,128]{4,3,2,1,0:T(8,128)S(1)}, f32[2,1,2,224,128]{4,3,2,1,0:T(8,128)S(1)}, u32[]{:S(2)}, u32[]{:S(2)}) collective-permute-start(f32[2,1,2,224,128]{4,3,2,1,0:T(8,128)S(1)} %fusion.32), channel_id=1, source_target_pairs={{0,64},{64,0},{8,72},{72,8},{16,80},{80,16},{24,88},{88,24},{32,96... | collective-permute-start | bytes 1376264 | tf_op jit(solution)/shard_map/ppermute | solution.py:18
  450.4 28.5 %collective-permute-start.19 = (f32[2,1,2,224,128]{4,3,2,1,0:T(8,128)S(1)}, f32[2,1,2,224,128]{4,3,2,1,0:T(8,128)S(1)}, u32[]{:S(2)}, u32[]{:S(2)}) collective-permute-start(f32[2,1,2,224,128]{4,3,2,1,0:T(8,128)S(1)} %fusion.35), channel_id=1, source_target_pairs={{0,128},{128,0},{8,136},{136,8},{16,144},{144,16},{24,152},{152,24... | collective-permute-start | bytes 1376264 | tf_op jit(solution)/shard_map/ppermute | solution.py:18
  (18 other events, 130.6 us)
Sparse Core Ops, SparseCore 0:
  238.6 39.8 reduce-scatter.2
  362.8 227.6 reduce-scatter.4
where the time goes:
time: 603 us; the launch traced here: 597 us
  waiting for transfers between devices  437 us (72%)
  starting transfers between devices  63.4 us (11%)
  other arithmetic  34 us (6%)
  matrix products  30.2 us (5%)
  between operations  15.8 us (3%)
  blocking collectives  13.8 us (2%)
    ppermute x20, waiting for transfers between devices, swapped(): return lax.ppermute(block, axis, route)  327 us
    reduce_scatter x1, waiting for transfers between devices, local(): lax.psum_scatter(lax.dot_general(full_gated, grad_out, (((0,), (0,)), (()...  110 us
    ppermute x20, starting transfers between devices, swapped(): return lax.ppermute(block, axis, route)  63.4 us
    dot_general x16, matrix products, apply_table(): return jnp.einsum(form, table, values, precision=HIGHEST)  24.2 us
    all_gather x1, blocking collectives, local(): full_gated = lax.all_gather(gated_out, 'chan', axis=1, tiled=True)  13.8 us
  transfers between devices with their start and end apart: 22, of which 20 were waited for; matrix products, arithmetic and copies ran while one was open for 4% of the time, Pallas kernels for 0%

commit v1 on v0

v1 whole, which is shorter than its diff:
```python
import jax
import jax.numpy as jnp
from jax import lax
from jax.experimental import pallas as pl
from jax.experimental.pallas import tpu as pltpu
from jax.sharding import PartitionSpec as P

VMEM_BYTES = 40 * 1024 * 1024


def partial_kernel(grad_ref, weight_ref, out_ref):
    for j in range(2):
        out_ref[j] = lax.dot_general(
            grad_ref[...],
            weight_ref[128 * j:128 * j + 128, :],
            (((1,), (1,)), ((), ())),
            preferred_element_type=jnp.float32,
        ).astype(jnp.bfloat16)


def partial_call(grad_out, out_weight):
    return pl.pallas_call(
        partial_kernel,
        out_shape=jax.ShapeDtypeStruct((8, 224, 128), jnp.bfloat16),
        grid=(4,),
        in_specs=[
            pl.BlockSpec((224, 1024), lambda i: (0, 0)),
            pl.BlockSpec((256, 1024), lambda i: (i, 0)),
        ],
        out_specs=pl.BlockSpec((2, 224, 128), lambda i: (i, 0, 0)),
        compiler_params=pltpu.CompilerParams(vmem_limit_bytes=VMEM_BYTES),
    )(grad_out, out_weight)


def pack_kernel(query_ref, key_ref, value_ref, filter_ref, partial_ref, send_ref, gated_ref):
    f32 = jnp.float32
    grad_gated = partial_ref[0].astype(f32)
    for j in range(1, 8):
        grad_gated = grad_gated + partial_ref[j].astype(f32)
    gated_ref[...] = grad_gated
    arrays = (
        key_ref[...].astype(f32) * value_ref[...].astype(f32),
        filter_ref[...],
        grad_gated * query_ref[...].astype(f32),
    )
    pad = jnp.zeros((16, 128), f32)
    for index, array in enumerate(arrays):
        for half in range(2):
            block = jnp.concatenate([array[112 * half:112 * half + 112], pad], axis=0).T
            for cc in range(4):
                row = (index * 2 + half) * 4 + cc
                send_ref[pl.ds(row, 32, stride=24), :] = block[32 * cc:32 * cc + 32]


def pack_call(query, key, value, filters, partials):
    return pl.pallas_call(
        pack_kernel,
        out_shape=(
            jax.ShapeDtypeStruct((768, 128), jnp.float32),
            jax.ShapeDtypeStruct((224, 128), jnp.float32),
        ),
        compiler_params=pltpu.CompilerParams(vmem_limit_bytes=VMEM_BYTES),
    )(query, key, value, filters, partials)


def conv_kernel(recv_ref, out_ref, xp, zp, fl, rh, rl, acc):
    f32, bf = jnp.float32, jnp.bfloat16
    row = lax.broadcasted_iota(jnp.int32, (16, 128), 0)
    lane = lax.broadcasted_iota(jnp.int32, (16, 128), 1)
    ri = lax.broadcasted_iota(jnp.int32, (64, 64), 0)
    ci = lax.broadcasted_iota(jnp.int32, (64, 64), 1)
    flip_blocks = jnp.where(ri + ci == 63, 1.0, 0.0).astype(bf)
    rows = lax.broadcasted_iota(jnp.int32, (128, 128), 0)
    cols = lax.broadcasted_iota(jnp.int32, (128, 128), 1)
    flip_lanes = jnp.where(rows + cols == 111, 1.0, 0.0).astype(bf)

    def split(block):
        high = block.astype(bf)
        return high, (block - high.astype(f32)).astype(bf)

    def flip(block):
        pair = jnp.concatenate(split(block), axis=0)
        turned = jnp.dot(pair, flip_lanes, preferred_element_type=f32).astype(bf)
        pair = jnp.concatenate([turned[0:64], turned[64:128]], axis=1)
        turned = jnp.dot(flip_blocks, pair, preferred_element_type=f32)
        return turned[:, 0:128] + turned[:, 128:256]

    xp[0:64, :] = jnp.zeros((64, 128), f32)
    zp[0:64, :] = jnp.zeros((64, 128), f32)
    for m in range(8):
        rh[128 * m + 112:128 * m + 128, :] = jnp.zeros((16, 1024), bf)
        rl[128 * m + 112:128 * m + 128, :] = jnp.zeros((16, 1024), bf)
    for d in range(2):
        acc[d, 0:8, :] = jnp.zeros((8, 1024), f32)
    fl[0:8, :] = jnp.zeros((8, 128), f32)

    for cc in range(4):
        for half in range(2):
            xp[pl.ds(64 + half, 32, stride=2), :] = recv_ref[pl.ds(half * 4 + cc, 32, stride=24), :]
            fl[pl.ds(8 + half, 32, stride=2), :] = recv_ref[pl.ds(8 + half * 4 + cc, 32, stride=24), :]
            zp[pl.ds(64 + half, 32, stride=2), :] = recv_ref[pl.ds(16 + half * 4 + cc, 32, stride=24), :]
        zp[64:128, :] = flip(zp[64:128, :])
        for k in range(64):
            m, r = k // 8, k % 8
            left = jnp.broadcast_to(fl[8 + k:9 + k, :], (16, 128))
            right = jnp.broadcast_to(pltpu.roll(fl[7 + k:8 + k, :], 16, 1), (16, 128))
            for p in range(7):
                src = jnp.where(lane < 128 - 16 * p - row, left, right)
                rolled = pltpu.roll(src, 16 * p, 1, stride=1, stride_axis=0)
                high, low = split(rolled)
                rh[128 * m + 16 * p:128 * m + 16 * p + 16, 128 * r:128 * r + 128] = high
                rl[128 * m + 16 * p:128 * m + 16 * p + 16, 128 * r:128 * r + 128] = low
        lhs = jnp.concatenate(
            [
                jnp.concatenate([ref[64 - 8 * m:128 - 8 * m, :] for m in range(8)], axis=1)
                for ref in (xp, zp)
            ],
            axis=0,
        )
        lhs_high, lhs_low = split(lhs)
        prod = (
            jnp.dot(lhs_high, rh[...], preferred_element_type=f32)
            + jnp.dot(lhs_low, rh[...], preferred_element_type=f32)
            + jnp.dot(lhs_high, rl[...], preferred_element_type=f32)
        )
        acc[0, 8:72, :] = prod[0:64]
        acc[1, 8:72, :] = prod[64:128]
        for d in range(2):
            total = acc[d, 8:72, 0:128]
            for r in range(1, 8):
                total = total + acc[d, 8 - r:72 - r, 128 * r:128 * r + 128]
            if d == 1:
                total = flip(total)
            xp[64:128, :] = total
            for half in range(2):
                out_ref[pl.ds((d * 2 + half) * 4 + cc, 32, stride=16), :] = xp[pl.ds(64 + half, 32, stride=2), :]

def conv_call(recv):
    f32, bf = jnp.float32, jnp.bfloat16
    return pl.pallas_call(
        conv_kernel,
        out_shape=jax.ShapeDtypeStruct((512, 128), f32),
        in_specs=[pl.BlockSpec(memory_space=pltpu.VMEM)],
        out_specs=pl.BlockSpec(memory_space=pltpu.VMEM),
        scratch_shapes=[
            pltpu.VMEM((128, 128), f32),
            pltpu.VMEM((128, 128), f32),
            pltpu.VMEM((72, 128), f32),
            pltpu.VMEM((1024, 1024), bf),
            pltpu.VMEM((1024, 1024), bf),
            pltpu.VMEM((2, 72, 1024), f32),
        ],
        compiler_params=pltpu.CompilerParams(vmem_limit_bytes=32 * 1024 * 1024),
    )(recv)


def unpack_kernel(recv_ref, query_ref, key_ref, value_ref, grad_ref, gated_ref, gq_ref, gk_ref, gv_ref):
    f32 = jnp.float32
    for half in range(2):
        rows = slice(112 * half, 112 * half + 112)
        blocks = []
        for index in range(2):
            pieces = [recv_ref[pl.ds((index * 2 + half) * 4 + cc, 32, stride=16), :] for cc in range(4)]
            blocks.append(jnp.concatenate(pieces, axis=0).T[0:112])
        conv_out, grad_mixed = blocks
        gated_ref[rows, :] = (query_ref[rows, :].astype(f32) * conv_out).astype(jnp.bfloat16)
        gq_ref[rows, :] = grad_ref[rows, :] * conv_out
        gk_ref[rows, :] = grad_mixed * value_ref[rows, :].astype(f32)
        gv_ref[rows, :] = grad_mixed * key_ref[rows, :].astype(f32)


def unpack_call(recv, query, key, value, grad_gated):
    grad = jax.ShapeDtypeStruct((224, 128), jnp.float32)
    return pl.pallas_call(
        unpack_kernel,
        out_shape=(jax.ShapeDtypeStruct((224, 128), jnp.bfloat16), grad, grad, grad),
        compiler_params=pltpu.CompilerParams(vmem_limit_bytes=VMEM_BYTES),
    )(recv, query, key, value, grad_gated)


def weight_kernel(gated_ref, grad_ref, out_ref, total):
    step = pl.program_id(0)
    part = lax.dot_general(
        gated_ref[0, 0], grad_ref[0], (((0,), (0,)), ((), ())), preferred_element_type=jnp.float32
    )

    @pl.when(step == 0)
    def _():
        total[...] = part

    @pl.when(step > 0)
    def _():
        total[...] += part

    @pl.when(step == 7)
    def _():
        out_ref[...] = total[...].astype(jnp.bfloat16)


def weight_call(gathered, grad_planes):
    return pl.pallas_call(
        weight_kernel,
        out_shape=jax.ShapeDtypeStruct((128, 1024), jnp.bfloat16),
        grid=(8,),
        in_specs=[
            pl.BlockSpec((1, 1, 224, 128), lambda i: (i, 1, 0, 0)),
            pl.BlockSpec((1, 224, 1024), lambda i: (i, 0, 0)),
        ],
        out_specs=pl.BlockSpec((128, 1024), lambda i: (0, 0)),
        scratch_shapes=[pltpu.VMEM((128, 1024), jnp.float32)],
        compiler_params=pltpu.CompilerParams(vmem_limit_bytes=VMEM_BYTES),
    )(gathered, grad_planes)


def layer_kernel(gated_ref, weight_ref, out_ref):
    full = jnp.concatenate([gated_ref[j, 0] for j in range(8)], axis=1)
    out_ref[...] = jnp.dot(full, weight_ref[...], preferred_element_type=jnp.float32)


def layer_call(gathered, out_weight):
    return pl.pallas_call(
        layer_kernel,
        out_shape=jax.ShapeDtypeStruct((224, 1024), jnp.float32),
        grid=(4,),
        in_specs=[
            pl.BlockSpec((8, 1, 224, 128), lambda i: (0, 0, 0, 0)),
            pl.BlockSpec((1024, 256), lambda i: (0, i)),
        ],
        out_specs=pl.BlockSpec((224, 256), lambda i: (0, i)),
        compiler_params=pltpu.CompilerParams(vmem_limit_bytes=VMEM_BYTES),
    )(gathered, out_weight)


def local(query_slab, key_slab, value_slab, filters, out_weight, grad_out):
    along_z = [[4 * z + y for z in range(8)] for y in range(4)]
    swap = [
        ((z * 4 + y) * 8 + j, (j * 4 + y) * 8 + z)
        for z in range(8)
        for y in range(4)
        for j in range(8)
    ]
    own_y = lax.axis_index("ctx") % 4
    grad_planes = lax.all_gather(grad_out, "ctx", axis=0, axis_index_groups=along_z)
    partials = partial_call(grad_out, out_weight)
    partials = lax.all_to_all(partials, "chan", 0, 0)
    sent, grad_gated = pack_call(query_slab, key_slab, value_slab, filters, partials)
    by_channel = lax.all_to_all(sent.reshape(32, 24, 128), "ctx", 0, 0).reshape(768, 128)
    convolved = conv_call(by_channel)
    by_token = lax.all_to_all(convolved.reshape(32, 16, 128), "ctx", 0, 0).reshape(512, 128)
    gated, grad_query, grad_key, grad_value = unpack_call(
        by_token, query_slab, key_slab, value_slab, grad_gated
    )
    swapped = lax.ppermute(gated, ("ctx", "chan"), swap)
    gathered = lax.all_gather(jnp.stack([gated, swapped]), "chan", axis=0)
    weight_part = weight_call(gathered, grad_planes).reshape(4, 32, 1024)
    total = lax.dynamic_index_in_dim(weight_part, own_y, 0, keepdims=False).astype(jnp.float32)
    arrived = []
    for step in range(1, 4):
        block = lax.dynamic_index_in_dim(weight_part, own_y ^ step, 0, keepdims=False)
        arrived.append(lax.ppermute(block, "ctx", [(i, i ^ step) for i in range(32)]))
    layer_out = layer_call(gathered, out_weight)
    for block in arrived:
        total = total + block.astype(jnp.float32)
    return (layer_out, grad_query, grad_key, grad_value, total)


def solution(mesh):
    placed = (
        P("ctx", "chan"),
        P("ctx", "chan"),
        P("ctx", "chan"),
        P("ctx", "chan"),
        P(None, "chan"),
        P("ctx", "chan"),
    )
    return jax.shard_map(
        local,
        mesh=mesh,
        in_specs=placed,
        out_specs=(
            P("ctx", "chan"),
            P("ctx", "chan"),
            P("ctx", "chan"),
            P("ctx", "chan"),
            P("ctx", "chan"),
        ),
        check_vma=False,
    )
```

time: 603 us -> 129 us (0.21)
  waiting for transfers between devices: 437 us -> 2.59 us
  blocking collectives: 13.8 us -> 81.5 us
  starting transfers between devices: 63.4 us -> 8.95 us
  other arithmetic: 34 us -> 1.54 us
  matrix products: 30.2 us -> 0 us
  Pallas kernels: 0 us -> 14.4 us
    ppermute x20 -> x4, waiting for transfers between devices: 327 us -> 1.91 us  [the longest x1 1.82 us: local(): swapped = lax.ppermute(gated, ('ctx', 'chan'), swap)]
    reduce_scatter x2 -> x0, waiting for transfers between devices: 110 us -> none  [the longest x1 110 us: local(): lax.psum_scatter(lax.dot_general(full_gated, grad_out, (((0,), (0,)), (()...]
    all_to_all x0 -> x3, blocking collectives: none -> 59.2 us  [the longest x1 29.1 us: local(): lax.all_to_all(sent.reshape(32, 24, 128), 'ctx', 0, 0).reshape(768, 128)]
    ppermute x20 -> x4, starting transfers between devices: 63.4 us -> 8.91 us  [the longest x1 5.66 us: local(): swapped = lax.ppermute(gated, ('ctx', 'chan'), swap)]
    dot_general x19 -> x0, matrix products: 30.2 us -> none  [the longest x16 24.2 us: apply_table(): return jnp.einsum(form, table, values, precision=HIGHEST)]
    select_n x20 -> x0, other arithmetic: 15.4 us -> none  [the longest x10 11.9 us: butterfly_forward(): spectrum = jnp.where(upper_half, high_value, low_value)]
    pallas_call x0 -> x6, Pallas kernels: none -> 14.4 us  [the longest x1 6.71 us: conv_call(): pl.pallas_call(conv_kernel, out_shape=jax.ShapeDtypeStruct((512, 128), f3...]
    sub x40 -> x0, other arithmetic: 12.3 us -> none  [the longest x10 8.63 us: butterfly_forward(): partner_block - spectrum]
  transfers between devices with their start and end apart: 22 -> 5, of which waited for: 20 -> 2; matrix products, arithmetic and copies ran while one was open for 4% -> 0% of each run, Pallas kernels for 0% -> 9%
where the time goes in v1:
time: 129 us; the launch traced here: 128 us
  blocking collectives  81.5 us (63%)
  Pallas kernels  14.4 us (11%)
  between operations  14.2 us (11%)
  starting transfers between devices  8.95 us (7%)
  local copies, waits for them, and re-layouts  5.32 us (4%)
  waiting for transfers between devices  2.59 us (2%)
  other arithmetic  1.54 us (1%)
    all_to_all x1, blocking collectives, local(): lax.all_to_all(sent.reshape(32, 24, 128), 'ctx', 0, 0).reshape(768, 128)  29.1 us
    all_gather x1, blocking collectives, local(): gathered = lax.all_gather(jnp.stack([gated, swapped]), 'chan', axis=0)  22.3 us
    all_to_all x1, blocking collectives, local(): lax.all_to_all(convolved.reshape(32, 16, 128), 'ctx', 0, 0)  15.7 us
    all_to_all x1, blocking collectives, local(): partials = lax.all_to_all(partials, 'chan', 0, 0)  14.4 us
    pallas_call x1, Pallas kernels, conv_call(): pl.pallas_call(conv_kernel, out_shape=jax.ShapeDtypeStruct((512, 128), f3...  6.71 us
    ppermute x1, starting transfers between devices, local(): swapped = lax.ppermute(gated, ('ctx', 'chan'), swap)  5.66 us
    unnamed x16, local copies, waits for them, and re-layouts  4.66 us
    ppermute x3, starting transfers between devices, local(): lax.ppermute(block, 'ctx', [(i, i ^ step) for i in range(32)])  3.25 us
  transfers between devices with their start and end apart: 5, of which 2 were waited for; matrix products, arithmetic and copies ran while one was open for 0% of the time, Pallas kernels for 9%

profile of v1, /device:TPU:1, one launch (start us, length us, event | category | flops | bytes accessed | tf_op | source)
XLA Modules:
  0.0 128.4 jit_solution(4824831865163905788)
XLA Ops:
  7.2 0.0 all-gather.4.cloned.1.call-start
  7.3 0.7 all-gather.4.cloned.1.call-update
  7.9 0.0 copy-start
  8.0 1.6 %copy-done = bf16[1024,1024]{1,0:T(8,128)(2,1)S(1)} copy-done((bf16[1024,1024]{1,0:T(8,128)(2,1)S(1)}, bf16[1024,1024]{1,0:T(8,128)(2,1)}, u32[]{:S(2)}) %copy-start) | copy-done | bytes 2097176
  9.5 1.0 copy-done.3
  10.6 1.6 %shard_map.101 = bf16[8,224,128]{2,1,0:T(8,128)(2,1)S(1)} custom-call(bf16[224,1024]{1,0:T(8,128)(2,1)S(1)} %copy-done.3, bf16[1024,1024]{1,0:T(8,128)(2,1)S(1)} %copy-done), custom_call_target="tpu_custom_call" | custom-call | tf_op jit(solution)/shard_map/pallas_call | solution.py:22
  12.2 14.4 %all_to_all.15.partial_ref = bf16[8,224,128]{2,1,0:T(8,128)(2,1)S(1)} all-to-all(bf16[8,224,128]{2,1,0:T(8,128)(2,1)S(1)} %shard_map.101), channel_id=1, replica_groups=mesh['ctx'=32,'chan'=8] {'chan'}, dimensions={0} | all-to-all | bytes 917504 | tf_op jit(solution)/shard_map/all_to_all | solution.py:245
  26.6 0.2 shard_map.102
  26.8 29.1 %all_to_all.16 = f32[32,24,128]{2,1,0:T(8,128)S(1)} all-to-all(f32[32,24,128]{2,1,0:T(8,128)S(1)} %bitcast.26), channel_id=1, replica_groups=mesh['ctx'=32,'chan'=8] {'ctx'}, dimensions={0} | all-to-all | bytes 786432 | tf_op jit(solution)/shard_map/all_to_all | solution.py:247
  55.9 6.7 %shard_map.103 = f32[512,128]{1,0:T(8,128)S(1)} custom-call(f32[768,128]{1,0:T(8,128)S(1)} %bitcast.21), custom_call_target="tpu_custom_call" | custom-call | tf_op jit(solution)/shard_map/pallas_call | solution.py:140
  62.6 15.7 %all_to_all.17 = f32[32,16,128]{2,1,0:T(8,128)S(1)} all-to-all(f32[32,16,128]{2,1,0:T(8,128)S(1)} %bitcast.25), channel_id=1, replica_groups=mesh['ctx'=32,'chan'=8] {'ctx'}, dimensions={0} | all-to-all | bytes 524288 | tf_op jit(solution)/shard_map/all_to_all | solution.py:249
  78.3 0.9 shard_map.104
  79.2 5.7 %collective-permute-start = (bf16[224,128]{1,0:T(8,128)(2,1)S(1)}, bf16[224,128]{1,0:T(8,128)(2,1)S(1)}, u32[]{:S(2)}, u32[]{:S(2)}) collective-permute-start(bf16[224,128]{1,0:T(8,128)(2,1)S(1)} %get-tuple-element.13), channel_id=1, source_target_pairs={{0,0},{1,32},{2,64},{3,96},{4,128},{5,160},{6,192},{7,224},{8,8},{... | collective-permute-start | bytes 172040 | tf_op jit(solution)/shard_map/ppermute | solution.py:253
  84.9 1.8 %collective-permute-done = bf16[224,128]{1,0:T(8,128)(2,1)S(1)} collective-permute-done((bf16[224,128]{1,0:T(8,128)(2,1)S(1)}, bf16[224,128]{1,0:T(8,128)(2,1)S(1)}, u32[]{:S(2)}, u32[]{:S(2)}) %collective-permute-start) | collective-permute-done | bytes 57376 | tf_op jit(solution)/shard_map/ppermute | solution.py:253
  86.7 22.3 %all-gather = bf16[16,224,128]{2,1,0:T(8,128)(2,1)S(1)} all-gather(bf16[2,224,128]{2,1,0:T(8,128)(2,1)S(1)} %pad_maximum_fusion), channel_id=2, replica_groups=mesh['ctx'=32,'chan'=8] {'chan'}, dimensions={0}, use_global_device_ids=true | all-gather | bytes 1032192 | tf_op jit(solution)/shard_map/all_gather | solution.py:254
  109.0 2.0 %copy-done.2 = bf16[1792,1024]{1,0:T(8,128)(2,1)S(1)} copy-done((bf16[1792,1024]{1,0:T(8,128)(2,1)S(1)}, bf16[1792,1024]{1,0:T(8,128)(2,1)}, u32[]{:S(2)}) %copy-start.2) | copy-done | bytes 3670040
  111.1 2.5 %shard_map.106 = bf16[128,1024]{1,0:T(8,128)(2,1)S(1)} custom-call(bf16[8,2,224,128]{3,2,1,0:T(8,128)(2,1)S(1)} %bitcast.18, bf16[8,224,1024]{2,1,0:T(8,128)(2,1)S(1)} %bitcast.20), custom_call_target="tpu_custom_call" | custom-call | tf_op jit(solution)/shard_map/pallas_call | solution.py:201
  113.5 0.7 dynamic-slice_bitcast_fusion.2
  114.2 0.0 collective-permute-start.1
  114.2 1.1 collective-permute-start.3
  115.3 2.1 %collective-permute-start.2 = (bf16[32,1024]{1,0:T(8,128)(2,1)S(1)}, bf16[32,1024]{1,0:T(8,128)(2,1)}, u32[]{:S(2)}, u32[]{:S(2)}) collective-permute-start(bf16[32,1024]{1,0:T(8,128)(2,1)S(1)} %get-tuple-element.19), channel_id=1, source_target_pairs={{0,16},{8,24},{16,0},{24,8},{32,48},{40,56},{48,32},{56,40},{64,80... | collective-permute-start | bytes 196616 | tf_op jit(solution)/shard_map/ppermute | solution.py:260
  117.5 2.5 %shard_map.105 = f32[224,1024]{1,0:T(8,128)} custom-call(bf16[8,2,224,128]{3,2,1,0:T(8,128)(2,1)S(1)} %bitcast.19, bf16[1024,1024]{1,0:T(8,128)(2,1)S(1)} %copy-done.1), custom_call_target="tpu_custom_call" | custom-call | tf_op jit(solution)/shard_map/pallas_call | solution.py:221
  120.0 0.1 collective-permute-done.2
  120.1 1.5 %fusion.1 = f32[32,1024]{1,0:T(8,128)} fusion(bf16[32,1024]{1,0:T(8,128)(2,1)S(1)} %collective-permute-done.3, bf16[32,1024]{1,0:T(8,128)(2,1)} %collective-permute-done.2, bf16[32,1024]{1,0:T(8,128)(2,1)S(1)} %collective-permute-done.1, bf16[4,32,1024]{2,1,0:T(8,128)(2,1)S(1)} %bitcast.23, s32[]{:T(128)S(6)} %select_n.21), kind=kLoop, calls=%fused_computation.2 | loop fusion | flops 229376 | bytes 393220 | tf_op jit(solution)/shard_map/add | solution.py:263
  (16 shorter events, 0.0 us)
Async XLA Ops:
  7.2 19.4 %copy-start.6 = (bf16[224,128]{1,0:T(8,128)(2,1)S(1)}, bf16[224,128]{1,0:T(8,128)(2,1)}, u32[]{:S(2)}) copy-start(bf16[224,128]{1,0:T(8,128)(2,1)} %value_ref.3) | copy-start | bytes 172036
  7.2 19.4 %copy-start.5 = (bf16[224,128]{1,0:T(8,128)(2,1)S(1)}, bf16[224,128]{1,0:T(8,128)(2,1)}, u32[]{:S(2)}) copy-start(bf16[224,128]{1,0:T(8,128)(2,1)} %key_ref.3) | copy-start | bytes 172036
  7.2 19.4 %copy-start.4 = (bf16[224,128]{1,0:T(8,128)(2,1)S(1)}, bf16[224,128]{1,0:T(8,128)(2,1)}, u32[]{:S(2)}) copy-start(bf16[224,128]{1,0:T(8,128)(2,1)} %query_ref.3) | copy-start | bytes 172036
  7.2 19.4 %copy-start.7 = (f32[224,128]{1,0:T(8,128)S(1)}, f32[224,128]{1,0:T(8,128)}, u32[]{:S(2)}) copy-start(f32[224,128]{1,0:T(8,128)} %filter_ref.1) | copy-start | bytes 344068
  7.2 101.8 %all-gather.4.cloned.1.call-start = ((), (), s32[]{:S(2)}) async-start(), calls=%async_computation.3 | async-start | bytes 4128768 | tf_op jit(solution)/shard_map/all_gather | solution.py:243
  7.9 1.6 %copy-start = (bf16[1024,1024]{1,0:T(8,128)(2,1)S(1)}, bf16[1024,1024]{1,0:T(8,128)(2,1)}, u32[]{:S(2)}) copy-start(bf16[1024,1024]{1,0:T(8,128)(2,1)} %weight_ref.3) | copy-start | bytes 6291460
  9.5 1.0 copy-start.3
  78.3 39.1 %copy-start.1 = (bf16[1024,1024]{1,0:T(8,128)(2,1)S(1)}, bf16[1024,1024]{1,0:T(8,128)(2,1)}, u32[]{:S(2)}) copy-start(bf16[1024,1024]{1,0:T(8,128)(2,1)} %weight_ref.3) | copy-start | bytes 6291460
  79.2 7.5 %collective-permute-start = (bf16[224,128]{1,0:T(8,128)(2,1)S(1)}, bf16[224,128]{1,0:T(8,128)(2,1)S(1)}, u32[]{:S(2)}, u32[]{:S(2)}) collective-permute-start(bf16[224,128]{1,0:T(8,128)(2,1)S(1)} %get-tuple-element.13), channel_id=1, source_target_pairs={{0,0},{1,32},{2,64},{3,96},{4,128},{5,160},{6,192},{7,224},{8,8},{... | collective-permute-start | bytes 172040 | tf_op jit(solution)/shard_map/ppermute | solution.py:253
  109.0 2.0 %copy-start.2 = (bf16[1792,1024]{1,0:T(8,128)(2,1)S(1)}, bf16[1792,1024]{1,0:T(8,128)(2,1)}, u32[]{:S(2)}) copy-start(bf16[1792,1024]{1,0:T(8,128)(2,1)} %all-gather.4.cloned.1.call-done) | copy-start | bytes 11010052
  114.2 5.8 %collective-permute-start.1 = (bf16[32,1024]{1,0:T(8,128)(2,1)}, bf16[32,1024]{1,0:T(8,128)(2,1)S(1)}, u32[]{:S(2)}, u32[]{:S(2)}) collective-permute-start(bf16[32,1024]{1,0:T(8,128)(2,1)} %get-tuple-element.17), channel_id=1, source_target_pairs={{0,8},{8,0},{16,24},{24,16},{32,40},{40,32},{48,56},{56,48},{64,72... | collective-permute-start | bytes 196616 | tf_op jit(solution)/shard_map/ppermute | solution.py:260
  114.2 5.8 %collective-permute-start.3 = (bf16[32,1024]{1,0:T(8,128)(2,1)S(1)}, bf16[32,1024]{1,0:T(8,128)(2,1)S(1)}, u32[]{:S(2)}, u32[]{:S(2)}) collective-permute-start(bf16[32,1024]{1,0:T(8,128)(2,1)S(1)} %get-tuple-element.18), channel_id=1, source_target_pairs={{0,24},{8,16},{16,8},{24,0},{32,56},{40,48},{48,40},{56,32},{64,88... | collective-permute-start | bytes 196616 | tf_op jit(solution)/shard_map/ppermute | solution.py:260
  115.3 4.7 %collective-permute-start.2 = (bf16[32,1024]{1,0:T(8,128)(2,1)S(1)}, bf16[32,1024]{1,0:T(8,128)(2,1)}, u32[]{:S(2)}, u32[]{:S(2)}) collective-permute-start(bf16[32,1024]{1,0:T(8,128)(2,1)S(1)} %get-tuple-element.19), channel_id=1, source_target_pairs={{0,16},{8,24},{16,0},{24,8},{32,48},{40,56},{48,32},{56,40},{64,80... | collective-permute-start | bytes 196616 | tf_op jit(solution)/shard_map/ppermute | solution.py:260
Sparse Core Ops, SparseCore 0:
  9.8 62.3 all-gather.3

commit v2 on v1

--- a/solution.py
+++ b/solution.py
@@ -5,30 +5,67 @@
 from jax.experimental.pallas import tpu as pltpu
 from jax.sharding import PartitionSpec as P
 
-VMEM_BYTES = 40 * 1024 * 1024
-
-
-def partial_kernel(grad_ref, weight_ref, out_ref):
-    for j in range(2):
-        out_ref[j] = lax.dot_general(
+VMEM_BYTES = 16 * 1024 * 1024
+WHOLE_BYTES = 60 * 1024 * 1024
+
+
+def partial_kernel(
+    grad_hbm, weight_hbm, out_hbm, grad_ref, weight_ref, out_ref, grad_sem, weight_sem, out_sem
+):
+    def grad_copy(part):
+        rows = pl.ds(112 * part, 112)
+        return pltpu.make_async_copy(grad_hbm.at[rows], grad_ref.at[rows], grad_sem.at[part])
+
+    def weight_copy(part):
+        rows = pl.ds(128 * part, 128)
+        return pltpu.make_async_copy(weight_hbm.at[rows], weight_ref.at[rows], weight_sem.at[part])
+
+    for part in range(2):
+        grad_copy(part).start()
+    for part in range(8):
+        weight_copy(part).start()
+    for part in range(2):
+        grad_copy(part).wait()
+    out_copies = []
+    for j in range(0, 8, 2):
+        weight_copy(j).wait()
+        weight_copy(j + 1).wait()
+        product = lax.dot_general(
             grad_ref[...],
-            weight_ref[128 * j:128 * j + 128, :],
+            weight_ref[128 * j:128 * j + 256, :],
             (((1,), (1,)), ((), ())),
             preferred_element_type=jnp.float32,
         ).astype(jnp.bfloat16)
+        out_ref[j] = product[:, 0:128]
+        out_ref[j + 1] = product[:, 128:256]
+        out_copies.append(
+            pltpu.make_async_copy(
+                out_ref.at[pl.ds(j, 2)], out_hbm.at[pl.ds(j, 2)], out_sem.at[j // 2]
+            )
+        )
+        out_copies[-1].start()
+    for copy in out_copies:
+        copy.wait()
 
 
 def partial_call(grad_out, out_weight):
     return pl.pallas_call(
         partial_kernel,
         out_shape=jax.ShapeDtypeStruct((8, 224, 128), jnp.bfloat16),
-        grid=(4,),
         in_specs=[
-            pl.BlockSpec((224, 1024), lambda i: (0, 0)),
-            pl.BlockSpec((256, 1024), lambda i: (i, 0)),
-        ],
-        out_specs=pl.BlockSpec((2, 224, 128), lambda i: (i, 0, 0)),
-        compiler_params=pltpu.CompilerParams(vmem_limit_bytes=VMEM_BYTES),
+            pl.BlockSpec(memory_space=pltpu.MemorySpace.HBM),
+            pl.BlockSpec(memory_space=pltpu.MemorySpace.HBM),
+        ],
+        out_specs=pl.BlockSpec(memory_space=pltpu.MemorySpace.HBM),
+        scratch_shapes=[
+            pltpu.VMEM((224, 1024), jnp.bfloat16),
+            pltpu.VMEM((1024, 1024), jnp.bfloat16),
+            pltpu.VMEM((8, 224, 128), jnp.bfloat16),
+            pltpu.SemaphoreType.DMA((2,)),
+            pltpu.SemaphoreType.DMA((8,)),
+            pltpu.SemaphoreType.DMA((4,)),
+        ],
+        compiler_params=pltpu.CompilerParams(vmem_limit_bytes=WHOLE_BYTES),
     )(grad_out, out_weight)
 
 
@@ -118,13 +155,15 @@
             axis=0,
         )
         lhs_high, lhs_low = split(lhs)
-        prod = (
-            jnp.dot(lhs_high, rh[...], preferred_element_type=f32)
-            + jnp.dot(lhs_low, rh[...], preferred_element_type=f32)
-            + jnp.dot(lhs_high, rl[...], preferred_element_type=f32)
-        )
-        acc[0, 8:72, :] = prod[0:64]
-        acc[1, 8:72, :] = prod[64:128]
+        for n in range(0, 1024, 256):
+            cols = slice(n, n + 256)
+            prod = (
+                jnp.dot(lhs_high, rh[:, cols], preferred_element_type=f32)
+                + jnp.dot(lhs_low, rh[:, cols], preferred_element_type=f32)
+                + jnp.dot(lhs_high, rl[:, cols], preferred_element_type=f32)
+            )
+            acc[0, 8:72, cols] = prod[0:64]
+            acc[1, 8:72, cols] = prod[64:128]
         for d in range(2):
             total = acc[d, 8:72, 0:128]
             for r in range(1, 8):
@@ -150,70 +189,150 @@
             pltpu.VMEM((1024, 1024), bf),
             pltpu.VMEM((2, 72, 1024), f32),
         ],
-        compiler_params=pltpu.CompilerParams(vmem_limit_bytes=32 * 1024 * 1024),
+        compiler_params=pltpu.CompilerParams(vmem_limit_bytes=VMEM_BYTES),
     )(recv)
 
 
-def unpack_kernel(recv_ref, query_ref, key_ref, value_ref, grad_ref, gated_ref, gq_ref, gk_ref, gv_ref):
+def unpack_kernel(
+    recv_ref, query_ref, key_ref, value_ref, grad_ref, send_ref, gated_hbm, gq_ref, gk_ref, gv_ref,
+    gated_ref, sem,
+):
     f32 = jnp.float32
+    pad = jnp.zeros((16, 128), f32)
+    gated_copies = []
     for half in range(2):
         rows = slice(112 * half, 112 * half + 112)
         blocks = []
         for index in range(2):
             pieces = [recv_ref[pl.ds((index * 2 + half) * 4 + cc, 32, stride=16), :] for cc in range(4)]
-            blocks.append(jnp.concatenate(pieces, axis=0).T[0:112])
-        conv_out, grad_mixed = blocks
-        gated_ref[rows, :] = (query_ref[rows, :].astype(f32) * conv_out).astype(jnp.bfloat16)
+            blocks.append(jnp.concatenate(pieces, axis=0))
+        conv_out = blocks[0].T[0:112]
+        grad_mixed = blocks[1].T[0:112]
+        query = query_ref[rows, :].astype(f32)
+        by_channel = jnp.concatenate([query, pad], axis=0).T * blocks[0]
+        by_channel = by_channel.astype(jnp.bfloat16)
+        for y in range(4):
+            for j in range(8):
+                send_ref[8 * y + j, 32 * half:32 * half + 32, :] = by_channel[32 * y:32 * y + 32]
+        gated_ref[rows, :] = (query * conv_out).astype(jnp.bfloat16)
         gq_ref[rows, :] = grad_ref[rows, :] * conv_out
+        gated_copy = pltpu.make_async_copy(
+            gated_ref.at[pl.ds(112 * half, 112)], gated_hbm.at[pl.ds(112 * half, 112)], sem.at[half]
+        )
+        gated_copy.start()
+        gated_copies.append(gated_copy)
         gk_ref[rows, :] = grad_mixed * value_ref[rows, :].astype(f32)
         gv_ref[rows, :] = grad_mixed * key_ref[rows, :].astype(f32)
+    for gated_copy in gated_copies:
+        gated_copy.wait()
 
 
 def unpack_call(recv, query, key, value, grad_gated):
+    bf = jnp.bfloat16
     grad = jax.ShapeDtypeStruct((224, 128), jnp.float32)
     return pl.pallas_call(
         unpack_kernel,
-        out_shape=(jax.ShapeDtypeStruct((224, 128), jnp.bfloat16), grad, grad, grad),
+        out_shape=(
+            jax.ShapeDtypeStruct((32, 64, 128), bf),
+            jax.ShapeDtypeStruct((224, 128), bf),
+            grad,
+            grad,
+            grad,
+        ),
+        out_specs=tuple(
+            pl.BlockSpec(memory_space=pltpu.MemorySpace.HBM if index == 1 else pltpu.VMEM)
+            for index in range(5)
+        ),
+        scratch_shapes=[
+            pltpu.VMEM((224, 128), bf),
+            pltpu.SemaphoreType.DMA((2,)),
+        ],
         compiler_params=pltpu.CompilerParams(vmem_limit_bytes=VMEM_BYTES),
     )(recv, query, key, value, grad_gated)
 
 
-def weight_kernel(gated_ref, grad_ref, out_ref, total):
-    step = pl.program_id(0)
-    part = lax.dot_general(
-        gated_ref[0, 0], grad_ref[0], (((0,), (0,)), ((), ())), preferred_element_type=jnp.float32
+def weight_kernel(
+    own_ref, gated_hbm, own, before, after, far_low, far_high, out_hbm,
+    gated_ref, rows_ref, out_ref, gated_sem, sem, out_sem,
+):
+    parts = (
+        (own, 0),
+        (own, 112),
+        (after, 0),
+        (after, 112),
+        (far_low, 0),
+        (far_high, 0),
+        (before, 0),
+        (before, 112),
     )
-
-    @pl.when(step == 0)
-    def _():
-        total[...] = part
-
-    @pl.when(step > 0)
-    def _():
-        total[...] += part
-
-    @pl.when(step == 7)
-    def _():
-        out_ref[...] = total[...].astype(jnp.bfloat16)
-
-
-def weight_call(gathered, grad_planes):
+    gated_copies, copies = [], []
+    for turn in range(4):
+        source = lax.rem(own_ref[0] + turn, 4)
+        gated_copies.append(
+            pltpu.make_async_copy(
+                gated_hbm.at[pl.ds(8 * source, 8)], gated_ref.at[turn], gated_sem.at[turn]
+            )
+        )
+        gated_copies[-1].start()
+        for index in (2 * turn, 2 * turn + 1):
+            source, start = parts[index]
+            copies.append(
+                pltpu.make_async_copy(
+                    source.at[pl.ds(start, 112)],
+                    rows_ref.at[pl.ds(128 * index, 112)],
+                    sem.at[index],
+                )
+            )
+            copies[-1].start()
+    for index in range(8):
+        rows_ref[128 * index + 112:128 * index + 128, :] = jnp.zeros((16, 1024), jnp.bfloat16)
+    lhs = []
+    for turn in range(4):
+        gated_copies[turn].wait()
+        copies[2 * turn].wait()
+        copies[2 * turn + 1].wait()
+        block = gated_ref[turn]
+        lhs.append(block[:, 0:32, :].reshape(256, 128))
+        lhs.append(block[:, 32:64, :].reshape(256, 128))
+    lhs = jnp.concatenate(lhs, axis=1)
+    out_copies = []
+    for n in range(4):
+        cols = pl.ds(256 * n, 256)
+        out_ref[:, 256 * n:256 * n + 256] = jnp.dot(
+            lhs, rows_ref[:, 256 * n:256 * n + 256], preferred_element_type=jnp.float32
+        ).astype(jnp.bfloat16)
+        out_copies.append(
+            pltpu.make_async_copy(out_ref.at[:, cols], out_hbm.at[:, cols], out_sem.at[n])
+        )
+        out_copies[-1].start()
+    for copy in out_copies:
+        copy.wait()
+
+
+def weight_call(own_y, gathered, parts):
+    hbm = pl.BlockSpec(memory_space=pltpu.MemorySpace.HBM)
     return pl.pallas_call(
         weight_kernel,
-        out_shape=jax.ShapeDtypeStruct((128, 1024), jnp.bfloat16),
-        grid=(8,),
-        in_specs=[
-            pl.BlockSpec((1, 1, 224, 128), lambda i: (i, 1, 0, 0)),
-            pl.BlockSpec((1, 224, 1024), lambda i: (i, 0, 0)),
-        ],
-        out_specs=pl.BlockSpec((128, 1024), lambda i: (0, 0)),
-        scratch_shapes=[pltpu.VMEM((128, 1024), jnp.float32)],
-        compiler_params=pltpu.CompilerParams(vmem_limit_bytes=VMEM_BYTES),
-    )(gathered, grad_planes)
+        out_shape=jax.ShapeDtypeStruct((256, 1024), jnp.bfloat16),
+        in_specs=[pl.BlockSpec(memory_space=pltpu.SMEM)] + [hbm] * 6,
+        out_specs=hbm,
+        scratch_shapes=[
+            pltpu.VMEM((4, 8, 64, 128), jnp.bfloat16),
+            pltpu.VMEM((1024, 1024), jnp.bfloat16),
+            pltpu.VMEM((256, 1024), jnp.bfloat16),
+            pltpu.SemaphoreType.DMA((4,)),
+            pltpu.SemaphoreType.DMA((8,)),
+            pltpu.SemaphoreType.DMA((4,)),
+        ],
+        compiler_params=pltpu.CompilerParams(vmem_limit_bytes=WHOLE_BYTES),
+        cost_estimate=pl.CostEstimate(
+            flops=2 * 256 * 896 * 1024, bytes_accessed=3 * 1024 * 1024, transcendentals=0
+        ),
+    )(own_y, gathered, *parts)
 
 
 def layer_kernel(gated_ref, weight_ref, out_ref):
-    full = jnp.concatenate([gated_ref[j, 0] for j in range(8)], axis=1)
+    full = jnp.concatenate([gated_ref[j] for j in range(8)], axis=1)
     out_ref[...] = jnp.dot(full, weight_ref[...], preferred_element_type=jnp.float32)
 
 
@@ -223,7 +342,7 @@
         out_shape=jax.ShapeDtypeStruct((224, 1024), jnp.float32),
         grid=(4,),
         in_specs=[
-            pl.BlockSpec((8, 1, 224, 128), lambda i: (0, 0, 0, 0)),
+            pl.BlockSpec((8, 224, 128), lambda i: (0, 0, 0)),
             pl.BlockSpec((1024, 256), lambda i: (0, i)),
         ],
         out_specs=pl.BlockSpec((224, 256), lambda i: (0, i)),
@@ -232,36 +351,37 @@
 
 
 def local(query_slab, key_slab, value_slab, filters, out_weight, grad_out):
+    up = [(4 * z + y, 4 * z + (y + 1) % 4) for z in range(8) for y in range(4)]
+    down = [(4 * z + y, 4 * z + (y + 3) % 4) for z in range(8) for y in range(4)]
     along_z = [[4 * z + y for z in range(8)] for y in range(4)]
-    swap = [
-        ((z * 4 + y) * 8 + j, (j * 4 + y) * 8 + z)
-        for z in range(8)
-        for y in range(4)
-        for j in range(8)
-    ]
-    own_y = lax.axis_index("ctx") % 4
-    grad_planes = lax.all_gather(grad_out, "ctx", axis=0, axis_index_groups=along_z)
+    planes = [list(range(32 * z, 32 * z + 32)) for z in range(8)]
+    together = lax.optimization_barrier
+    own_y = (lax.axis_index("ctx") % 4).astype(jnp.int32).reshape(1)
+    before = lax.ppermute(grad_out, "ctx", up)
+    after = lax.ppermute(grad_out, "ctx", down)
     partials = partial_call(grad_out, out_weight)
     partials = lax.all_to_all(partials, "chan", 0, 0)
+    before, after, own_y, partials = together((before, after, own_y, partials))
     sent, grad_gated = pack_call(query_slab, key_slab, value_slab, filters, partials)
     by_channel = lax.all_to_all(sent.reshape(32, 24, 128), "ctx", 0, 0).reshape(768, 128)
+    before, after, by_channel = together((before, after, by_channel))
+    far_low = lax.ppermute(after[0:112], "ctx", down)
+    far_high = lax.ppermute(before[112:224], "ctx", up)
     convolved = conv_call(by_channel)
+    far_low, far_high, convolved = together((far_low, far_high, convolved))
     by_token = lax.all_to_all(convolved.reshape(32, 16, 128), "ctx", 0, 0).reshape(512, 128)
-    gated, grad_query, grad_key, grad_value = unpack_call(
+    plane_sent, gated, grad_query, grad_key, grad_value = unpack_call(
         by_token, query_slab, key_slab, value_slab, grad_gated
     )
-    swapped = lax.ppermute(gated, ("ctx", "chan"), swap)
-    gathered = lax.all_gather(jnp.stack([gated, swapped]), "chan", axis=0)
-    weight_part = weight_call(gathered, grad_planes).reshape(4, 32, 1024)
-    total = lax.dynamic_index_in_dim(weight_part, own_y, 0, keepdims=False).astype(jnp.float32)
-    arrived = []
-    for step in range(1, 4):
-        block = lax.dynamic_index_in_dim(weight_part, own_y ^ step, 0, keepdims=False)
-        arrived.append(lax.ppermute(block, "ctx", [(i, i ^ step) for i in range(32)]))
-    layer_out = layer_call(gathered, out_weight)
-    for block in arrived:
-        total = total + block.astype(jnp.float32)
-    return (layer_out, grad_query, grad_key, grad_value, total)
+    plane_gated = lax.all_to_all(plane_sent, ("ctx", "chan"), 0, 0, axis_index_groups=planes)
+    weight_part = weight_call(
+        own_y, plane_gated, (grad_out, before, after, far_low, far_high)
+    ).reshape(8, 32, 1024)
+    arrived = lax.all_to_all(weight_part, "ctx", 0, 0, axis_index_groups=along_z)
+    full_gated = lax.all_gather(gated, "chan", axis=0)
+    layer_out = layer_call(full_gated, out_weight)
+    grad_weight = jnp.sum(arrived.astype(jnp.float32), axis=0)
+    return (layer_out, grad_query, grad_key, grad_value, grad_weight)
 
 
 def solution(mesh):

time: 129 us -> 117 us (0.907)
  between operations: 14.2 us -> 0.82 us
  blocking collectives: 81.5 us -> 71.1 us
  waiting for transfers between devices: 2.59 us -> 10.8 us
  starting transfers between devices: 8.95 us -> 15.2 us
  local copies, waits for them, and re-layouts: 5.32 us -> 0.07 us
  Pallas kernels: 14.4 us -> 17.7 us
    all_to_all x0 -> x2, waiting for transfers between devices: none -> 10.8 us  [the longest x1 8.78 us: local(): partials = lax.all_to_all(partials, 'chan', 0, 0)]
    all_gather x1, blocking collectives: 22.3 us -> 13.3 us  [local(): full_gated = lax.all_gather(gated, 'chan', axis=0)]
    all_to_all x0 -> x2, starting transfers between devices: none -> 8.77 us  [the longest x1 5.26 us: local(): partials = lax.all_to_all(partials, 'chan', 0, 0)]
    unnamed x16 -> x18, local copies, waits for them, and re-layouts: 4.66 us -> 0.04 us
    all_to_all x1, blocking collectives: 14.4 us -> 18.8 us  [local(): lax.all_to_all(plane_sent, ('ctx', 'chan'), 0, 0, axis_index_groups=planes)]
    all_to_all x1, blocking collectives: 29.1 us -> 24.8 us  [local(): lax.all_to_all(sent.reshape(32, 24, 128), 'ctx', 0, 0).reshape(768, 128)]
    ppermute x4, starting transfers between devices: 8.91 us -> 6.4 us  [the longest x1 3.64 us: local(): after = lax.ppermute(grad_out, 'ctx', down)]
    pallas_call x1, Pallas kernels: 1.64 us -> 4.12 us  [partial_call(): pl.pallas_call(partial_kernel, out_shape=jax.ShapeDtypeStruct((8, 224, 12...]
  transfers between devices with their start and end apart: 5 -> 6, of which waited for: 2 -> 2; matrix products, arithmetic and copies ran while one was open for 0% -> 0% of each run, Pallas kernels for 9% -> 11%
where the time goes in v2:
time: 117 us; the launch traced here: 116 us
  blocking collectives  71.1 us (61%)
  Pallas kernels  17.7 us (15%)
  starting transfers between devices  15.2 us (13%)
  waiting for transfers between devices  10.8 us (9%)
    all_to_all x1, blocking collectives, local(): lax.all_to_all(sent.reshape(32, 24, 128), 'ctx', 0, 0).reshape(768, 128)  24.8 us
    all_to_all x1, blocking collectives, local(): lax.all_to_all(plane_sent, ('ctx', 'chan'), 0, 0, axis_index_groups=planes)  18.8 us
    all_to_all x1, blocking collectives, local(): lax.all_to_all(convolved.reshape(32, 16, 128), 'ctx', 0, 0)  14.1 us
    all_gather x1, blocking collectives, local(): full_gated = lax.all_gather(gated, 'chan', axis=0)  13.3 us
    all_to_all x1, waiting for transfers between devices, local(): partials = lax.all_to_all(partials, 'chan', 0, 0)  8.78 us
    pallas_call x1, Pallas kernels, conv_call(): pl.pallas_call(conv_kernel, out_shape=jax.ShapeDtypeStruct((512, 128), f3...  6.4 us
    all_to_all x1, starting transfers between devices, local(): partials = lax.all_to_all(partials, 'chan', 0, 0)  5.26 us
    pallas_call x1, Pallas kernels, partial_call(): pl.pallas_call(partial_kernel, out_shape=jax.ShapeDtypeStruct((8, 224, 12...  4.12 us
  transfers between devices with their start and end apart: 6, of which 2 were waited for; matrix products, arithmetic and copies ran while one was open for 0% of the time, Pallas kernels for 11%

profile of v2, /device:TPU:1, one launch (start us, length us, event | category | flops | bytes accessed | tf_op | source)
XLA Modules:
  0.0 116.4 jit_solution(11941630757897387049)
XLA Ops:
  0.7 3.6 %collective-permute-start.1 = (bf16[224,1024]{1,0:T(8,128)(2,1)}, bf16[224,1024]{1,0:T(8,128)(2,1)S(1)}, u32[]{:S(2)}, u32[]{:S(2)}) collective-permute-start(bf16[224,1024]{1,0:T(8,128)(2,1)} %own.1), channel_id=1, source_target_pairs={{0,24},{8,0},{16,8},{24,16},{32,56},{40,32},{48,40},{56,48},{64,88... | collective-permute-start | bytes 1376264 | tf_op jit(solution)/shard_map/ppermute | solution.py:361
  4.3 0.0 collective-permute-start
  4.3 4.1 %shard_map.101 = bf16[8,224,128]{2,1,0:T(8,128)(2,1)} custom-call(bf16[224,1024]{1,0:T(8,128)(2,1)} %own.1, bf16[1024,1024]{1,0:T(8,128)(2,1)} %weight_ref.1), custom_call_target="tpu_custom_call" | custom-call | tf_op jit(solution)/shard_map/pallas_call | solution.py:52
  8.4 5.3 %all-to-all-start = ((bf16[8,224,128]{2,1,0:T(8,128)(2,1)}), bf16[8,224,128]{2,1,0:T(8,128)(2,1)S(1)}, u32[]{:S(2)}, u32[]{:S(2)}) async-start(bf16[8,224,128]{2,1,0:T(8,128)(2,1)} %shard_map.101), calls=%async_computation | async-start | bytes 917504 | tf_op jit(solution)/shard_map/all_to_all | solution.py:363
  13.7 8.8 %all-to-all-done.partial_ref = bf16[8,224,128]{2,1,0:T(8,128)(2,1)S(1)} async-done(((bf16[8,224,128]{2,1,0:T(8,128)(2,1)}), bf16[8,224,128]{2,1,0:T(8,128)(2,1)S(1)}, u32[]{:S(2)}, u32[]{:S(2)}) %all-to-all-start) | async-done | bytes 458784 | tf_op jit(solution)/shard_map/all_to_all | solution.py:363
  22.5 0.0 collective-permute-done.1.after
  22.5 0.0 copy-start.6
  22.5 0.2 shard_map.102
  22.7 24.8 %all_to_all.25 = f32[32,24,128]{2,1,0:T(8,128)S(1)} all-to-all(f32[32,24,128]{2,1,0:T(8,128)S(1)} %bitcast.11), channel_id=1, replica_groups=mesh['ctx'=32,'chan'=8] {'ctx'}, dimensions={0} | all-to-all | bytes 786432 | tf_op jit(solution)/shard_map/all_to_all | solution.py:366
  47.6 0.2 collective-permute-start.3
  47.8 2.5 %collective-permute-start.2 = (bf16[112,1024]{1,0:T(8,128)(2,1)S(1)}, bf16[112,1024]{1,0:T(8,128)(2,1)S(1)}, u32[]{:S(2)}, u32[]{:S(2)}) collective-permute-start(bf16[112,1024]{1,0:T(8,128)(2,1)S(1)} %slice.6), channel_id=1, source_target_pairs={{0,24},{8,0},{16,8},{24,16},{32,56},{40,32},{48,40},{56,48},{64,88... | collective-permute-start | bytes 688136 | tf_op jit(solution)/shard_map/ppermute | solution.py:368
  50.4 6.4 %shard_map.103 = f32[512,128]{1,0:T(8,128)S(1)} custom-call(f32[768,128]{1,0:T(8,128)S(1)} %bitcast.8), custom_call_target="tpu_custom_call" | custom-call | tf_op jit(solution)/shard_map/pallas_call | solution.py:179
  56.8 0.0 collective-permute-done.3.far_high
  56.8 0.0 collective-permute-done.2.far_low
  56.8 14.1 %all_to_all.26 = f32[32,16,128]{2,1,0:T(8,128)S(1)} all-to-all(f32[32,16,128]{2,1,0:T(8,128)S(1)} %bitcast.9), channel_id=1, replica_groups=mesh['ctx'=32,'chan'=8] {'ctx'}, dimensions={0} | all-to-all | bytes 524288 | tf_op jit(solution)/shard_map/all_to_all | solution.py:372
  70.9 1.0 shard_map.104
  72.0 18.8 %all_to_all.27.gated_hbm = bf16[32,64,128]{2,1,0:T(8,128)(2,1)} all-to-all(bf16[32,64,128]{2,1,0:T(8,128)(2,1)S(1)} %get-tuple-element.36), channel_id=1, replica_groups={{0,1,2,3,4,5,6,7,8,9,10,11,12,13,14,15,16,17,18,19,20,21,22,23,24,25,26..., dimensions={0} | all-to-all | bytes 1048576 | tf_op jit(solution)/shard_map/all_to_all | solution.py:376
  90.8 0.0 copy-start
  90.8 3.4 %shard_map.106 = bf16[256,1024]{1,0:T(8,128)(2,1)} custom-call(s32[1]{0:T(128)} %bitcast.own_ref, bf16[32,64,128]{2,1,0:T(8,128)(2,1)} %all_to_all.27.gated_hbm, bf16[224,1024]{1,0:T(8,128)(2,1)} %own.1, bf16[224,1024]{1,0:T(8,128)(2,1)} %copy-done.6, bf16[224,1024]{1,0:T(8,128)(2,1)} %copy-done.5, bf16[112,1024]{1,0:T(8,128)(2,1)} %copy-done.8, ...), custom_call_target="tpu_custom_call" | custom-call | flops 469762048 | bytes 3145728 | tf_op jit(solution)/shard_map/pallas_call | solution.py:314
  94.3 3.5 %all-to-all-start.4 = ((bf16[8,32,1024]{2,1,0:T(8,128)(2,1)}), bf16[8,32,1024]{2,1,0:T(8,128)(2,1)S(1)}, u32[]{:S(2)}, u32[]{:S(2)}) async-start(bf16[8,32,1024]{2,1,0:T(8,128)(2,1)} %bitcast.12), calls=%async_computation.4 | async-start | bytes 1048576 | tf_op jit(solution)/shard_map/all_to_all | solution.py:380
  97.8 13.3 %all-gather = bf16[1792,128]{1,0:T(8,128)(2,1)S(1)} all-gather(bf16[224,128]{1,0:T(8,128)(2,1)S(1)} %get-tuple-element.31), channel_id=2, replica_groups=mesh['ctx'=32,'chan'=8] {'chan'}, dimensions={0}, use_global_device_ids=true | all-gather | bytes 516096 | tf_op jit(solution)/shard_map/all_gather | solution.py:381
  111.1 2.5 %shard_map.105 = f32[224,1024]{1,0:T(8,128)} custom-call(bf16[8,224,128]{2,1,0:T(8,128)(2,1)S(1)} %bitcast.7, bf16[1024,1024]{1,0:T(8,128)(2,1)S(1)} %copy-done), custom_call_target="tpu_custom_call" | custom-call | tf_op jit(solution)/shard_map/pallas_call | solution.py:340
  113.6 2.1 %all-to-all-done.4 = bf16[8,32,1024]{2,1,0:T(8,128)(2,1)S(1)} async-done(((bf16[8,32,1024]{2,1,0:T(8,128)(2,1)}), bf16[8,32,1024]{2,1,0:T(8,128)(2,1)S(1)}, u32[]{:S(2)}, u32[]{:S(2)}) %all-to-all-start.4) | async-done | bytes 524320 | tf_op jit(solution)/shard_map/all_to_all | solution.py:380
  115.7 0.7 convert_reduce_fusion
  (19 shorter events, 0.1 us)
Async XLA Ops:
  0.6 21.9 %copy-start.3 = (bf16[224,128]{1,0:T(8,128)(2,1)S(1)}, bf16[224,128]{1,0:T(8,128)(2,1)}, u32[]{:S(2)}) copy-start(bf16[224,128]{1,0:T(8,128)(2,1)} %value_ref.3) | copy-start | bytes 172036
  0.6 21.9 %copy-start.2 = (bf16[224,128]{1,0:T(8,128)(2,1)S(1)}, bf16[224,128]{1,0:T(8,128)(2,1)}, u32[]{:S(2)}) copy-start(bf16[224,128]{1,0:T(8,128)(2,1)} %key_ref.3) | copy-start | bytes 172036
  0.7 21.9 %copy-start.1 = (bf16[224,128]{1,0:T(8,128)(2,1)S(1)}, bf16[224,128]{1,0:T(8,128)(2,1)}, u32[]{:S(2)}) copy-start(bf16[224,128]{1,0:T(8,128)(2,1)} %query_ref.3) | copy-start | bytes 172036
  0.7 21.9 %copy-start.4 = (f32[224,128]{1,0:T(8,128)S(1)}, f32[224,128]{1,0:T(8,128)}, u32[]{:S(2)}) copy-start(f32[224,128]{1,0:T(8,128)} %filter_ref.1) | copy-start | bytes 344068
  0.7 21.8 %collective-permute-start.1 = (bf16[224,1024]{1,0:T(8,128)(2,1)}, bf16[224,1024]{1,0:T(8,128)(2,1)S(1)}, u32[]{:S(2)}, u32[]{:S(2)}) collective-permute-start(bf16[224,1024]{1,0:T(8,128)(2,1)} %own.1), channel_id=1, source_target_pairs={{0,24},{8,0},{16,8},{24,16},{32,56},{40,32},{48,40},{56,48},{64,88... | collective-permute-start | bytes 1376264 | tf_op jit(solution)/shard_map/ppermute | solution.py:361
  4.3 18.2 %collective-permute-start = (bf16[224,1024]{1,0:T(8,128)(2,1)}, bf16[224,1024]{1,0:T(8,128)(2,1)S(1)}, u32[]{:S(2)}, u32[]{:S(2)}) collective-permute-start(bf16[224,1024]{1,0:T(8,128)(2,1)} %own.1), channel_id=1, source_target_pairs={{0,8},{8,16},{16,24},{24,0},{32,40},{40,48},{48,56},{56,32},{64,72... | collective-permute-start | bytes 1376264 | tf_op jit(solution)/shard_map/ppermute | solution.py:360
  8.4 14.0 %all-to-all-start = ((bf16[8,224,128]{2,1,0:T(8,128)(2,1)}), bf16[8,224,128]{2,1,0:T(8,128)(2,1)S(1)}, u32[]{:S(2)}, u32[]{:S(2)}) async-start(bf16[8,224,128]{2,1,0:T(8,128)(2,1)} %shard_map.101), calls=%async_computation | async-start | bytes 917504 | tf_op jit(solution)/shard_map/all_to_all | solution.py:363
  22.5 68.3 %copy-start.5 = (bf16[224,1024]{1,0:T(8,128)(2,1)}, bf16[224,1024]{1,0:T(8,128)(2,1)S(1)}, u32[]{:S(2)}) copy-start(bf16[224,1024]{1,0:T(8,128)(2,1)S(1)} %collective-permute-done.1.after) | copy-start | bytes 1376260
  22.5 68.3 %copy-start.6 = (bf16[224,1024]{1,0:T(8,128)(2,1)}, bf16[224,1024]{1,0:T(8,128)(2,1)S(1)}, u32[]{:S(2)}) copy-start(bf16[224,1024]{1,0:T(8,128)(2,1)S(1)} %collective-permute-done.before) | copy-start | bytes 1376260
  47.6 9.2 %collective-permute-start.3 = (bf16[112,1024]{1,0:T(8,128)(2,1)S(1)}, bf16[112,1024]{1,0:T(8,128)(2,1)S(1)}, u32[]{:S(2)}, u32[]{:S(2)}) collective-permute-start(bf16[112,1024]{1,0:T(8,128)(2,1)S(1)} %slice.7), channel_id=1, source_target_pairs={{0,8},{8,16},{16,24},{24,0},{32,40},{40,48},{48,56},{56,32},{64,72... | collective-permute-start | bytes 688136 | tf_op jit(solution)/shard_map/ppermute | solution.py:369
  47.8 9.0 %collective-permute-start.2 = (bf16[112,1024]{1,0:T(8,128)(2,1)S(1)}, bf16[112,1024]{1,0:T(8,128)(2,1)S(1)}, u32[]{:S(2)}, u32[]{:S(2)}) collective-permute-start(bf16[112,1024]{1,0:T(8,128)(2,1)S(1)} %slice.6), channel_id=1, source_target_pairs={{0,24},{8,0},{16,8},{24,16},{32,56},{40,32},{48,40},{56,48},{64,88... | collective-permute-start | bytes 688136 | tf_op jit(solution)/shard_map/ppermute | solution.py:368
  56.8 34.0 %copy-start.7 = (bf16[112,1024]{1,0:T(8,128)(2,1)}, bf16[112,1024]{1,0:T(8,128)(2,1)S(1)}, u32[]{:S(2)}) copy-start(bf16[112,1024]{1,0:T(8,128)(2,1)S(1)} %collective-permute-done.3.far_high) | copy-start | bytes 688132
  56.8 34.0 %copy-start.8 = (bf16[112,1024]{1,0:T(8,128)(2,1)}, bf16[112,1024]{1,0:T(8,128)(2,1)S(1)}, u32[]{:S(2)}) copy-start(bf16[112,1024]{1,0:T(8,128)(2,1)S(1)} %collective-permute-done.2.far_low) | copy-start | bytes 688132
  90.8 20.3 %copy-start = (bf16[1024,1024]{1,0:T(8,128)(2,1)S(1)}, bf16[1024,1024]{1,0:T(8,128)(2,1)}, u32[]{:S(2)}) copy-start(bf16[1024,1024]{1,0:T(8,128)(2,1)} %weight_ref.1) | copy-start | bytes 6291460
  94.3 21.4 %all-to-all-start.4 = ((bf16[8,32,1024]{2,1,0:T(8,128)(2,1)}), bf16[8,32,1024]{2,1,0:T(8,128)(2,1)S(1)}, u32[]{:S(2)}, u32[]{:S(2)}) async-start(bf16[8,32,1024]{2,1,0:T(8,128)(2,1)} %bitcast.12), calls=%async_computation.4 | async-start | bytes 1048576 | tf_op jit(solution)/shard_map/all_to_all | solution.py:380

commit v3 on v2

--- a/solution.py
+++ b/solution.py
@@ -251,101 +251,71 @@
     )(recv, query, key, value, grad_gated)
 
 
-def weight_kernel(
-    own_ref, gated_hbm, own, before, after, far_low, far_high, out_hbm,
-    gated_ref, rows_ref, out_ref, gated_sem, sem, out_sem,
-):
+def weight_kernel(own_ref, gated_ref, own, before, after, far_low, far_high, out_ref):
     parts = (
-        (own, 0),
-        (own, 112),
-        (after, 0),
-        (after, 112),
-        (far_low, 0),
-        (far_high, 0),
-        (before, 0),
-        (before, 112),
-    )
-    gated_copies, copies = [], []
-    for turn in range(4):
-        source = lax.rem(own_ref[0] + turn, 4)
-        gated_copies.append(
-            pltpu.make_async_copy(
-                gated_hbm.at[pl.ds(8 * source, 8)], gated_ref.at[turn], gated_sem.at[turn]
+        (own, 0, 0, 0),
+        (own, 112, 0, 1),
+        (after, 0, 1, 0),
+        (after, 112, 1, 1),
+        (far_low, 0, 2, 0),
+        (far_high, 0, 2, 1),
+        (before, 0, 3, 0),
+        (before, 112, 3, 1),
+    )
+    lhs = []
+    for rows, start, turn, half in parts:
+        block = gated_ref[pl.ds(8 * lax.rem(own_ref[0] + turn, 4), 8)]
+        lhs.append(block[:, 32 * half:32 * half + 32, :].reshape(256, 128)[:, 0:112])
+    for n in range(4):
+        lanes = slice(256 * n, 256 * n + 256)
+        total = None
+        for gated, (rows, start, turn, half) in zip(lhs, parts):
+            product = jnp.dot(
+                gated, rows[start:start + 112, lanes], preferred_element_type=jnp.float32
             )
-        )
-        gated_copies[-1].start()
-        for index in (2 * turn, 2 * turn + 1):
-            source, start = parts[index]
-            copies.append(
-                pltpu.make_async_copy(
-                    source.at[pl.ds(start, 112)],
-                    rows_ref.at[pl.ds(128 * index, 112)],
-                    sem.at[index],
-                )
-            )
-            copies[-1].start()
-    for index in range(8):
-        rows_ref[128 * index + 112:128 * index + 128, :] = jnp.zeros((16, 1024), jnp.bfloat16)
-    lhs = []
-    for turn in range(4):
-        gated_copies[turn].wait()
-        copies[2 * turn].wait()
-        copies[2 * turn + 1].wait()
-        block = gated_ref[turn]
-        lhs.append(block[:, 0:32, :].reshape(256, 128))
-        lhs.append(block[:, 32:64, :].reshape(256, 128))
-    lhs = jnp.concatenate(lhs, axis=1)
-    out_copies = []
+            total = product if total is None else total + product
+        out_ref[:, lanes] = total.astype(jnp.bfloat16)
+
+
+def weight_call(own_y, gathered, parts):
+    vmem = pl.BlockSpec(memory_space=pltpu.VMEM)
+    return pl.pallas_call(
+        weight_kernel,
+        out_shape=jax.ShapeDtypeStruct((256, 1024), jnp.bfloat16),
+        in_specs=[pl.BlockSpec(memory_space=pltpu.SMEM)] + [vmem] * 6,
+        out_specs=vmem,
+        compiler_params=pltpu.CompilerParams(vmem_limit_bytes=VMEM_BYTES),
+        cost_estimate=pl.CostEstimate(
+            flops=2 * 256 * 896 * 1024, bytes_accessed=3 * 1024 * 1024, transcendentals=0
+        ),
+    )(own_y, gathered, *parts)
+
+
+def layer_kernel(gated_ref, weight_ref, out_hbm, out_ref, sem):
+    full = jnp.concatenate([gated_ref[j] for j in range(8)], axis=1)
+    copies = []
     for n in range(4):
         cols = pl.ds(256 * n, 256)
         out_ref[:, 256 * n:256 * n + 256] = jnp.dot(
-            lhs, rows_ref[:, 256 * n:256 * n + 256], preferred_element_type=jnp.float32
-        ).astype(jnp.bfloat16)
-        out_copies.append(
-            pltpu.make_async_copy(out_ref.at[:, cols], out_hbm.at[:, cols], out_sem.at[n])
+            full, weight_ref[:, 256 * n:256 * n + 256], preferred_element_type=jnp.float32
         )
-        out_copies[-1].start()
-    for copy in out_copies:
+        copies.append(pltpu.make_async_copy(out_ref.at[:, cols], out_hbm.at[:, cols], sem.at[n]))
+        copies[-1].start()
+    for copy in copies:
         copy.wait()
 
 
-def weight_call(own_y, gathered, parts):
-    hbm = pl.BlockSpec(memory_space=pltpu.MemorySpace.HBM)
-    return pl.pallas_call(
-        weight_kernel,
-        out_shape=jax.ShapeDtypeStruct((256, 1024), jnp.bfloat16),
-        in_specs=[pl.BlockSpec(memory_space=pltpu.SMEM)] + [hbm] * 6,
-        out_specs=hbm,
-        scratch_shapes=[
-            pltpu.VMEM((4, 8, 64, 128), jnp.bfloat16),
-            pltpu.VMEM((1024, 1024), jnp.bfloat16),
-            pltpu.VMEM((256, 1024), jnp.bfloat16),
-            pltpu.SemaphoreType.DMA((4,)),
-            pltpu.SemaphoreType.DMA((8,)),
-            pltpu.SemaphoreType.DMA((4,)),
-        ],
-        compiler_params=pltpu.CompilerParams(vmem_limit_bytes=WHOLE_BYTES),
-        cost_estimate=pl.CostEstimate(
-            flops=2 * 256 * 896 * 1024, bytes_accessed=3 * 1024 * 1024, transcendentals=0
-        ),
-    )(own_y, gathered, *parts)
-
-
-def layer_kernel(gated_ref, weight_ref, out_ref):
-    full = jnp.concatenate([gated_ref[j] for j in range(8)], axis=1)
-    out_ref[...] = jnp.dot(full, weight_ref[...], preferred_element_type=jnp.float32)
-
-
 def layer_call(gathered, out_weight):
+    vmem = pl.BlockSpec(memory_space=pltpu.VMEM)
     return pl.pallas_call(
         layer_kernel,
         out_shape=jax.ShapeDtypeStruct((224, 1024), jnp.float32),
-        grid=(4,),
-        in_specs=[
-            pl.BlockSpec((8, 224, 128), lambda i: (0, 0, 0)),
-            pl.BlockSpec((1024, 256), lambda i: (0, i)),
-        ],
-        out_specs=pl.BlockSpec((224, 256), lambda i: (0, i)),
+        in_specs=[vmem, vmem],
+        out_specs=pl.BlockSpec(memory_space=pltpu.MemorySpace.HBM),
+        scratch_shapes=[
+            pltpu.VMEM((224, 1024), jnp.float32),
+            pltpu.SemaphoreType.DMA((4,)),
+        ],
         compiler_params=pltpu.CompilerParams(vmem_limit_bytes=VMEM_BYTES),
     )(gathered, out_weight)
 
@@ -357,12 +327,13 @@
     planes = [list(range(32 * z, 32 * z + 32)) for z in range(8)]
     together = lax.optimization_barrier
     own_y = (lax.axis_index("ctx") % 4).astype(jnp.int32).reshape(1)
-    before = lax.ppermute(grad_out, "ctx", up)
-    after = lax.ppermute(grad_out, "ctx", down)
     partials = partial_call(grad_out, out_weight)
+    own_grad, own_y, partials = together((grad_out, own_y, partials))
     partials = lax.all_to_all(partials, "chan", 0, 0)
-    before, after, own_y, partials = together((before, after, own_y, partials))
+    before = lax.ppermute(own_grad, "ctx", up)
+    after = lax.ppermute(own_grad, "ctx", down)
     sent, grad_gated = pack_call(query_slab, key_slab, value_slab, filters, partials)
+    before, after, sent = together((before, after, sent))
     by_channel = lax.all_to_all(sent.reshape(32, 24, 128), "ctx", 0, 0).reshape(768, 128)
     before, after, by_channel = together((before, after, by_channel))
     far_low = lax.ppermute(after[0:112], "ctx", down)

time: 117 us -> 115 us (0.983)
  blocking collectives: 71.1 us -> 84.9 us
  waiting for transfers between devices: 10.8 us -> 3.11 us
  starting transfers between devices: 15.2 us -> 9.89 us
  Pallas kernels: 17.7 us -> 15.3 us
    all_to_all x0 -> x1, blocking collectives: none -> 14 us  [local(): partials = lax.all_to_all(partials, 'chan', 0, 0)]
    all_to_all x1 -> x0, waiting for transfers between devices: 8.78 us -> none  [local(): partials = lax.all_to_all(partials, 'chan', 0, 0)]
    all_to_all x1 -> x0, starting transfers between devices: 5.26 us -> none  [local(): partials = lax.all_to_all(partials, 'chan', 0, 0)]
    pallas_call x1, Pallas kernels: 3.43 us -> 2.02 us  [weight_call(): pl.pallas_call(weight_kernel, out_shape=jax.ShapeDtypeStruct((256, 1024),...]
  transfers between devices with their start and end apart: 6 -> 5, of which waited for: 2 -> 1; matrix products, arithmetic and copies ran while one was open for 0% -> 0% of each run, Pallas kernels for 11% -> 7%
where the time goes in v3:
time: 115 us
  blocking collectives  84.9 us (74%)
  Pallas kernels  15.3 us (13%)
  starting transfers between devices  9.89 us (9%)
  waiting for transfers between devices  3.11 us (3%)
    all_to_all x1, blocking collectives, local(): lax.all_to_all(sent.reshape(32, 24, 128), 'ctx', 0, 0).reshape(768, 128)  24.8 us
    all_to_all x1, blocking collectives, local(): lax.all_to_all(plane_sent, ('ctx', 'chan'), 0, 0, axis_index_groups=planes)  18.7 us
    all_to_all x1, blocking collectives, local(): lax.all_to_all(convolved.reshape(32, 16, 128), 'ctx', 0, 0)  14.2 us
    all_to_all x1, blocking collectives, local(): partials = lax.all_to_all(partials, 'chan', 0, 0)  14 us
    all_gather x1, blocking collectives, local(): full_gated = lax.all_gather(gated, 'chan', axis=0)  13.3 us
    pallas_call x1, Pallas kernels, conv_call(): pl.pallas_call(conv_kernel, out_shape=jax.ShapeDtypeStruct((512, 128), f3...  6.41 us
    pallas_call x1, Pallas kernels, partial_call(): pl.pallas_call(partial_kernel, out_shape=jax.ShapeDtypeStruct((8, 224, 12...  4.17 us
    ppermute x1, starting transfers between devices, local(): after = lax.ppermute(own_grad, 'ctx', down)  3.64 us
  transfers between devices with their start and end apart: 5, of which 1 were waited for; matrix products, arithmetic and copies ran while one was open for 0% of the time, Pallas kernels for 7%

profile of v3, /device:TPU:1, one launch (start us, length us, event | category | flops | bytes accessed | tf_op | source)
XLA Modules:
  0.0 114.8 jit_solution(11782199796830457224)
XLA Ops:
  0.6 0.0 copy-start.1
  0.6 0.0 copy-start.4
  0.7 4.2 %shard_map.101 = bf16[8,224,128]{2,1,0:T(8,128)(2,1)} custom-call(bf16[224,1024]{1,0:T(8,128)(2,1)} %own.1, bf16[1024,1024]{1,0:T(8,128)(2,1)} %weight_ref.1), custom_call_target="tpu_custom_call" | custom-call | tf_op jit(solution)/shard_map/pallas_call | solution.py:52
  4.9 3.6 %collective-permute-start.1 = (bf16[224,1024]{1,0:T(8,128)(2,1)S(1)}, bf16[224,1024]{1,0:T(8,128)(2,1)S(1)}, u32[]{:S(2)}, u32[]{:S(2)}) collective-permute-start(bf16[224,1024]{1,0:T(8,128)(2,1)S(1)} %copy-done.1), channel_id=1, source_target_pairs={{0,24},{8,0},{16,8},{24,16},{32,56},{40,32},{48,40},{56,48},{64,88... | collective-permute-start | bytes 1376264 | tf_op jit(solution)/shard_map/ppermute | solution.py:334
  8.5 0.0 collective-permute-start
  8.5 14.0 %all_to_all.25.partial_ref = bf16[8,224,128]{2,1,0:T(8,128)(2,1)S(1)} all-to-all(bf16[8,224,128]{2,1,0:T(8,128)(2,1)} %shard_map.101), channel_id=1, replica_groups=mesh['ctx'=32,'chan'=8] {'chan'}, dimensions={0} | all-to-all | bytes 917504 | tf_op jit(solution)/shard_map/all_to_all | solution.py:332
  22.5 0.2 shard_map.102
  22.7 0.0 collective-permute-done.1.after
  22.7 0.0 collective-permute-done.before
  22.7 24.8 %all_to_all.26 = f32[32,24,128]{2,1,0:T(8,128)S(1)} all-to-all(f32[32,24,128]{2,1,0:T(8,128)S(1)} %bitcast.11), channel_id=1, replica_groups=mesh['ctx'=32,'chan'=8] {'ctx'}, dimensions={0} | all-to-all | bytes 786432 | tf_op jit(solution)/shard_map/all_to_all | solution.py:337
  47.5 0.1 collective-permute-start.3
  47.6 2.7 %collective-permute-start.2 = (bf16[112,1024]{1,0:T(8,128)(2,1)S(1)}, bf16[112,1024]{1,0:T(8,128)(2,1)S(1)}, u32[]{:S(2)}, u32[]{:S(2)}) collective-permute-start(bf16[112,1024]{1,0:T(8,128)(2,1)S(1)} %slice.6), channel_id=1, source_target_pairs={{0,24},{8,0},{16,8},{24,16},{32,56},{40,32},{48,40},{56,48},{64,88... | collective-permute-start | bytes 688136 | tf_op jit(solution)/shard_map/ppermute | solution.py:339
  50.3 6.4 %shard_map.103 = f32[512,128]{1,0:T(8,128)S(1)} custom-call(f32[768,128]{1,0:T(8,128)S(1)} %bitcast.8), custom_call_target="tpu_custom_call" | custom-call | tf_op jit(solution)/shard_map/pallas_call | solution.py:179
  56.7 0.0 collective-permute-done.3.far_high
  56.7 0.0 collective-permute-done.2.far_low
  56.7 14.2 %all_to_all.27 = f32[32,16,128]{2,1,0:T(8,128)S(1)} all-to-all(f32[32,16,128]{2,1,0:T(8,128)S(1)} %bitcast.9), channel_id=1, replica_groups=mesh['ctx'=32,'chan'=8] {'ctx'}, dimensions={0} | all-to-all | bytes 524288 | tf_op jit(solution)/shard_map/all_to_all | solution.py:343
  70.9 1.0 shard_map.104
  71.9 18.7 %all_to_all.28.gated_ref = bf16[32,64,128]{2,1,0:T(8,128)(2,1)S(1)} all-to-all(bf16[32,64,128]{2,1,0:T(8,128)(2,1)S(1)} %get-tuple-element.40), channel_id=1, replica_groups={{0,1,2,3,4,5,6,7,8,9,10,11,12,13,14,15,16,17,18,19,20,21,22,23,24,25,26..., dimensions={0} | all-to-all | bytes 1048576 | tf_op jit(solution)/shard_map/all_to_all | solution.py:347
  90.7 2.0 %shard_map.106 = bf16[256,1024]{1,0:T(8,128)(2,1)} custom-call(s32[1]{0:T(128)} %bitcast.own_ref, bf16[32,64,128]{2,1,0:T(8,128)(2,1)S(1)} %all_to_all.28.gated_ref, bf16[224,1024]{1,0:T(8,128)(2,1)S(1)} %copy-done.1, bf16[224,1024]{1,0:T(8,128)(2,1)S(1)} %collective-permute-done.before, bf16[224,1024]{1,0:T(8,128)(2,1)S(1)} %collective-permute-done.1.after, ...), custom_call_target="tpu_custom_call" | custom-call | flops 469762048 | bytes 3145728 | tf_op jit(solution)/shard_map/pallas_call | solution.py:282
  92.7 3.5 %all-to-all-start.4 = ((bf16[8,32,1024]{2,1,0:T(8,128)(2,1)}), bf16[8,32,1024]{2,1,0:T(8,128)(2,1)S(1)}, u32[]{:S(2)}, u32[]{:S(2)}) async-start(bf16[8,32,1024]{2,1,0:T(8,128)(2,1)} %bitcast.6), calls=%async_computation.4 | async-start | bytes 1048576 | tf_op jit(solution)/shard_map/all_to_all | solution.py:351
  96.2 13.3 %all-gather = bf16[1792,128]{1,0:T(8,128)(2,1)S(1)} all-gather(bf16[224,128]{1,0:T(8,128)(2,1)S(1)} %get-tuple-element.35), channel_id=2, replica_groups=mesh['ctx'=32,'chan'=8] {'chan'}, dimensions={0}, use_global_device_ids=true | all-gather | bytes 516096 | tf_op jit(solution)/shard_map/all_gather | solution.py:352
  109.5 1.4 %shard_map.105 = f32[224,1024]{1,0:T(8,128)} custom-call(bf16[8,224,128]{2,1,0:T(8,128)(2,1)S(1)} %bitcast.7, bf16[1024,1024]{1,0:T(8,128)(2,1)S(1)} %copy-done), custom_call_target="tpu_custom_call" | custom-call | tf_op jit(solution)/shard_map/pallas_call | solution.py:310
  111.0 3.1 %all-to-all-done.4 = bf16[8,32,1024]{2,1,0:T(8,128)(2,1)S(1)} async-done(((bf16[8,32,1024]{2,1,0:T(8,128)(2,1)}), bf16[8,32,1024]{2,1,0:T(8,128)(2,1)S(1)}, u32[]{:S(2)}, u32[]{:S(2)}) %all-to-all-start.4) | async-done | bytes 524320 | tf_op jit(solution)/shard_map/all_to_all | solution.py:351
  114.1 0.7 convert_reduce_fusion
  (12 shorter events, 0.1 us)
Async XLA Ops:
  0.6 4.2 %copy-start.1 = (bf16[224,1024]{1,0:T(8,128)(2,1)S(1)}, bf16[224,1024]{1,0:T(8,128)(2,1)}, u32[]{:S(2)}) copy-start(bf16[224,1024]{1,0:T(8,128)(2,1)} %own.1) | copy-start | bytes 1376260
  0.6 21.9 %copy-start.4 = (bf16[224,128]{1,0:T(8,128)(2,1)S(1)}, bf16[224,128]{1,0:T(8,128)(2,1)}, u32[]{:S(2)}) copy-start(bf16[224,128]{1,0:T(8,128)(2,1)} %value_ref.3) | copy-start | bytes 172036
  0.7 21.9 %copy-start.3 = (bf16[224,128]{1,0:T(8,128)(2,1)S(1)}, bf16[224,128]{1,0:T(8,128)(2,1)}, u32[]{:S(2)}) copy-start(bf16[224,128]{1,0:T(8,128)(2,1)} %key_ref.3) | copy-start | bytes 172036
  0.7 21.9 %copy-start.2 = (bf16[224,128]{1,0:T(8,128)(2,1)S(1)}, bf16[224,128]{1,0:T(8,128)(2,1)}, u32[]{:S(2)}) copy-start(bf16[224,128]{1,0:T(8,128)(2,1)} %query_ref.3) | copy-start | bytes 172036
  0.7 21.9 %copy-start.5 = (f32[224,128]{1,0:T(8,128)S(1)}, f32[224,128]{1,0:T(8,128)}, u32[]{:S(2)}) copy-start(f32[224,128]{1,0:T(8,128)} %filter_ref.1) | copy-start | bytes 344068
  4.9 17.8 %collective-permute-start.1 = (bf16[224,1024]{1,0:T(8,128)(2,1)S(1)}, bf16[224,1024]{1,0:T(8,128)(2,1)S(1)}, u32[]{:S(2)}, u32[]{:S(2)}) collective-permute-start(bf16[224,1024]{1,0:T(8,128)(2,1)S(1)} %copy-done.1), channel_id=1, source_target_pairs={{0,24},{8,0},{16,8},{24,16},{32,56},{40,32},{48,40},{56,48},{64,88... | collective-permute-start | bytes 1376264 | tf_op jit(solution)/shard_map/ppermute | solution.py:334
  8.5 14.2 %collective-permute-start = (bf16[224,1024]{1,0:T(8,128)(2,1)S(1)}, bf16[224,1024]{1,0:T(8,128)(2,1)S(1)}, u32[]{:S(2)}, u32[]{:S(2)}) collective-permute-start(bf16[224,1024]{1,0:T(8,128)(2,1)S(1)} %copy-done.1), channel_id=1, source_target_pairs={{0,8},{8,16},{16,24},{24,0},{32,40},{40,48},{48,56},{56,32},{64,72... | collective-permute-start | bytes 1376264 | tf_op jit(solution)/shard_map/ppermute | solution.py:333
  47.5 9.2 %collective-permute-start.3 = (bf16[112,1024]{1,0:T(8,128)(2,1)S(1)}, bf16[112,1024]{1,0:T(8,128)(2,1)S(1)}, u32[]{:S(2)}, u32[]{:S(2)}) collective-permute-start(bf16[112,1024]{1,0:T(8,128)(2,1)S(1)} %slice.7), channel_id=1, source_target_pairs={{0,8},{8,16},{16,24},{24,0},{32,40},{40,48},{48,56},{56,32},{64,72... | collective-permute-start | bytes 688136 | tf_op jit(solution)/shard_map/ppermute | solution.py:340
  47.6 9.1 %collective-permute-start.2 = (bf16[112,1024]{1,0:T(8,128)(2,1)S(1)}, bf16[112,1024]{1,0:T(8,128)(2,1)S(1)}, u32[]{:S(2)}, u32[]{:S(2)}) collective-permute-start(bf16[112,1024]{1,0:T(8,128)(2,1)S(1)} %slice.6), channel_id=1, source_target_pairs={{0,24},{8,0},{16,8},{24,16},{32,56},{40,32},{48,40},{56,48},{64,88... | collective-permute-start | bytes 688136 | tf_op jit(solution)/shard_map/ppermute | solution.py:339
  90.7 18.8 %copy-start = (bf16[1024,1024]{1,0:T(8,128)(2,1)S(1)}, bf16[1024,1024]{1,0:T(8,128)(2,1)}, u32[]{:S(2)}) copy-start(bf16[1024,1024]{1,0:T(8,128)(2,1)} %weight_ref.1) | copy-start | bytes 6291460
  92.7 21.4 %all-to-all-start.4 = ((bf16[8,32,1024]{2,1,0:T(8,128)(2,1)}), bf16[8,32,1024]{2,1,0:T(8,128)(2,1)S(1)}, u32[]{:S(2)}, u32[]{:S(2)}) async-start(bf16[8,32,1024]{2,1,0:T(8,128)(2,1)} %bitcast.6), calls=%async_computation.4 | async-start | bytes 1048576 | tf_op jit(solution)/shard_map/all_to_all | solution.py:351

commit v4 on v3

--- a/solution.py
+++ b/solution.py
@@ -69,39 +69,47 @@
     )(grad_out, out_weight)
 
 
-def pack_kernel(query_ref, key_ref, value_ref, filter_ref, partial_ref, send_ref, gated_ref):
+def pack_kernel(query_ref, key_ref, value_ref, filter_ref, partial_ref, send_ref, gated_ref, s1):
     f32 = jnp.float32
     grad_gated = partial_ref[0].astype(f32)
     for j in range(1, 8):
         grad_gated = grad_gated + partial_ref[j].astype(f32)
     gated_ref[...] = grad_gated
-    arrays = (
-        key_ref[...].astype(f32) * value_ref[...].astype(f32),
-        filter_ref[...],
-        grad_gated * query_ref[...].astype(f32),
-    )
+    mixed = key_ref[...].astype(f32) * value_ref[...].astype(f32)
+    pieces = []
+    for array in (mixed, filter_ref[...]):
+        high = array.astype(jnp.bfloat16).astype(f32)
+        pieces += [high, array - high]
+    pieces.append(grad_gated * query_ref[...].astype(f32))
     pad = jnp.zeros((16, 128), f32)
-    for index, array in enumerate(arrays):
+    for index, array in enumerate(pieces):
         for half in range(2):
             block = jnp.concatenate([array[112 * half:112 * half + 112], pad], axis=0).T
             for cc in range(4):
                 row = (index * 2 + half) * 4 + cc
-                send_ref[pl.ds(row, 32, stride=24), :] = block[32 * cc:32 * cc + 32]
+                s1[pl.ds(row, 32, stride=40), :] = block[32 * cc:32 * cc + 32]
+    send_ref[...] = s1[...].astype(jnp.bfloat16)
 
 
 def pack_call(query, key, value, filters, partials):
     return pl.pallas_call(
         pack_kernel,
         out_shape=(
-            jax.ShapeDtypeStruct((768, 128), jnp.float32),
+            jax.ShapeDtypeStruct((1280, 128), jnp.bfloat16),
             jax.ShapeDtypeStruct((224, 128), jnp.float32),
         ),
+        scratch_shapes=[pltpu.VMEM((1280, 128), jnp.float32)],
         compiler_params=pltpu.CompilerParams(vmem_limit_bytes=VMEM_BYTES),
     )(query, key, value, filters, partials)
 
 
-def conv_kernel(recv_ref, out_ref, xp, zp, fl, rh, rl, acc):
+def conv_kernel(recv_ref, out_ref, s1, xp, zp, fl, rh, rl, acc):
     f32, bf = jnp.float32, jnp.bfloat16
+    s1[...] = recv_ref[...].astype(f32)
+
+    def piece(index, half, cc):
+        return s1[pl.ds((index * 2 + half) * 4 + cc, 32, stride=40), :]
+
     row = lax.broadcasted_iota(jnp.int32, (16, 128), 0)
     lane = lax.broadcasted_iota(jnp.int32, (16, 128), 1)
     ri = lax.broadcasted_iota(jnp.int32, (64, 64), 0)
@@ -133,9 +141,9 @@
 
     for cc in range(4):
         for half in range(2):
-            xp[pl.ds(64 + half, 32, stride=2), :] = recv_ref[pl.ds(half * 4 + cc, 32, stride=24), :]
-            fl[pl.ds(8 + half, 32, stride=2), :] = recv_ref[pl.ds(8 + half * 4 + cc, 32, stride=24), :]
-            zp[pl.ds(64 + half, 32, stride=2), :] = recv_ref[pl.ds(16 + half * 4 + cc, 32, stride=24), :]
+            xp[pl.ds(64 + half, 32, stride=2), :] = piece(0, half, cc) + piece(1, half, cc)
+            fl[pl.ds(8 + half, 32, stride=2), :] = piece(2, half, cc) + piece(3, half, cc)
+            zp[pl.ds(64 + half, 32, stride=2), :] = piece(4, half, cc)
         zp[64:128, :] = flip(zp[64:128, :])
         for k in range(64):
             m, r = k // 8, k % 8
@@ -182,6 +190,7 @@
         in_specs=[pl.BlockSpec(memory_space=pltpu.VMEM)],
         out_specs=pl.BlockSpec(memory_space=pltpu.VMEM),
         scratch_shapes=[
+            pltpu.VMEM((1280, 128), f32),
             pltpu.VMEM((128, 128), f32),
             pltpu.VMEM((128, 128), f32),
             pltpu.VMEM((72, 128), f32),
@@ -251,7 +260,7 @@
     )(recv, query, key, value, grad_gated)
 
 
-def weight_kernel(own_ref, gated_ref, own, before, after, far_low, far_high, out_ref):
+def weight_kernel(own_ref, gated_ref, own, before, after, far_low, far_high, out_hbm, out_ref, sem):
     parts = (
         (own, 0, 0, 0),
         (own, 112, 0, 1),
@@ -264,9 +273,12 @@
     )
     lhs = []
     for rows, start, turn, half in parts:
-        block = gated_ref[pl.ds(8 * lax.rem(own_ref[0] + turn, 4), 8)]
-        lhs.append(block[:, 32 * half:32 * half + 32, :].reshape(256, 128)[:, 0:112])
+        plane = 8 * lax.rem(own_ref[0] + turn, 4)
+        blocks = [gated_ref[plane + j][32 * half:32 * half + 32, :] for j in range(8)]
+        lhs.append(jnp.concatenate(blocks, axis=0)[:, 0:112])
+    copies = []
     for n in range(4):
+        cols = pl.ds(256 * n, 256)
         lanes = slice(256 * n, 256 * n + 256)
         total = None
         for gated, (rows, start, turn, half) in zip(lhs, parts):
@@ -275,6 +287,10 @@
             )
             total = product if total is None else total + product
         out_ref[:, lanes] = total.astype(jnp.bfloat16)
+        copies.append(pltpu.make_async_copy(out_ref.at[:, cols], out_hbm.at[:, cols], sem.at[n]))
+        copies[-1].start()
+    for copy in copies:
+        copy.wait()
 
 
 def weight_call(own_y, gathered, parts):
@@ -283,7 +299,11 @@
         weight_kernel,
         out_shape=jax.ShapeDtypeStruct((256, 1024), jnp.bfloat16),
         in_specs=[pl.BlockSpec(memory_space=pltpu.SMEM)] + [vmem] * 6,
-        out_specs=vmem,
+        out_specs=pl.BlockSpec(memory_space=pltpu.MemorySpace.HBM),
+        scratch_shapes=[
+            pltpu.VMEM((256, 1024), jnp.bfloat16),
+            pltpu.SemaphoreType.DMA((4,)),
+        ],
         compiler_params=pltpu.CompilerParams(vmem_limit_bytes=VMEM_BYTES),
         cost_estimate=pl.CostEstimate(
             flops=2 * 256 * 896 * 1024, bytes_accessed=3 * 1024 * 1024, transcendentals=0
@@ -291,33 +311,40 @@
     )(own_y, gathered, *parts)
 
 
-def layer_kernel(gated_ref, weight_ref, out_hbm, out_ref, sem):
-    full = jnp.concatenate([gated_ref[j] for j in range(8)], axis=1)
+def layer_kernel(own_ref, pair_0, pair_1, pair_2, pair_3, weight_ref, out_hbm, out_ref, sem):
+    chip, core = lax.div(own_ref[0], 2), lax.rem(own_ref[0], 2)
+    blocks, starts = [], []
+    for turn, pair in enumerate((pair_0, pair_1, pair_2, pair_3)):
+        base = 256 * lax.rem(chip + turn, 4)
+        for side in range(2):
+            blocks.append(pair[side])
+            starts.append(pl.multiple_of(base + 128 * lax.rem(core + side, 2), 128))
+    full = jnp.concatenate(blocks, axis=1)
     copies = []
     for n in range(4):
         cols = pl.ds(256 * n, 256)
-        out_ref[:, 256 * n:256 * n + 256] = jnp.dot(
-            full, weight_ref[:, 256 * n:256 * n + 256], preferred_element_type=jnp.float32
-        )
+        lanes = slice(256 * n, 256 * n + 256)
+        weight = jnp.concatenate([weight_ref[pl.ds(start, 128), lanes] for start in starts], axis=0)
+        out_ref[:, lanes] = jnp.dot(full, weight, preferred_element_type=jnp.float32)
         copies.append(pltpu.make_async_copy(out_ref.at[:, cols], out_hbm.at[:, cols], sem.at[n]))
         copies[-1].start()
     for copy in copies:
         copy.wait()
 
 
-def layer_call(gathered, out_weight):
+def layer_call(own_chan, pairs, out_weight):
     vmem = pl.BlockSpec(memory_space=pltpu.VMEM)
     return pl.pallas_call(
         layer_kernel,
         out_shape=jax.ShapeDtypeStruct((224, 1024), jnp.float32),
-        in_specs=[vmem, vmem],
+        in_specs=[pl.BlockSpec(memory_space=pltpu.SMEM)] + [vmem] * 5,
         out_specs=pl.BlockSpec(memory_space=pltpu.MemorySpace.HBM),
         scratch_shapes=[
             pltpu.VMEM((224, 1024), jnp.float32),
             pltpu.SemaphoreType.DMA((4,)),
         ],
         compiler_params=pltpu.CompilerParams(vmem_limit_bytes=VMEM_BYTES),
-    )(gathered, out_weight)
+    )(own_chan, *pairs, out_weight)
 
 
 def local(query_slab, key_slab, value_slab, filters, out_weight, grad_out):
@@ -328,13 +355,14 @@
     together = lax.optimization_barrier
     own_y = (lax.axis_index("ctx") % 4).astype(jnp.int32).reshape(1)
     partials = partial_call(grad_out, out_weight)
-    own_grad, own_y, partials = together((grad_out, own_y, partials))
+    own_chan = lax.axis_index("chan").astype(jnp.int32).reshape(1)
+    own_grad, own_y, own_chan, partials = together((grad_out, own_y, own_chan, partials))
     partials = lax.all_to_all(partials, "chan", 0, 0)
     before = lax.ppermute(own_grad, "ctx", up)
     after = lax.ppermute(own_grad, "ctx", down)
     sent, grad_gated = pack_call(query_slab, key_slab, value_slab, filters, partials)
     before, after, sent = together((before, after, sent))
-    by_channel = lax.all_to_all(sent.reshape(32, 24, 128), "ctx", 0, 0).reshape(768, 128)
+    by_channel = lax.all_to_all(sent.reshape(32, 40, 128), "ctx", 0, 0).reshape(1280, 128)
     before, after, by_channel = together((before, after, by_channel))
     far_low = lax.ppermute(after[0:112], "ctx", down)
     far_high = lax.ppermute(before[112:224], "ctx", up)
@@ -348,9 +376,15 @@
     weight_part = weight_call(
         own_y, plane_gated, (grad_out, before, after, far_low, far_high)
     ).reshape(8, 32, 1024)
+    gated, weight_part = together((gated, weight_part))
     arrived = lax.all_to_all(weight_part, "ctx", 0, 0, axis_index_groups=along_z)
-    full_gated = lax.all_gather(gated, "chan", axis=0)
-    layer_out = layer_call(full_gated, out_weight)
+    other = lax.ppermute(gated, "chan", [(i, i ^ 1) for i in range(8)])
+    pair = jnp.stack([gated, other])
+    pairs = [pair]
+    for turn in range(1, 4):
+        route = [((i + 2 * turn) % 8, i) for i in range(8)]
+        pairs.append(lax.ppermute(pair, "chan", route))
+    layer_out = layer_call(own_chan, pairs, out_weight)
     grad_weight = jnp.sum(arrived.astype(jnp.float32), axis=0)
     return (layer_out, grad_query, grad_key, grad_value, grad_weight)
 

time: 115 us -> 114 us (level)
  blocking collectives: 84.9 us -> 70.1 us
  waiting for transfers between devices: 3.11 us -> 12.8 us
  starting transfers between devices: 9.89 us -> 13.5 us
    all_gather x1 -> x0, blocking collectives: 13.3 us -> none  [local(): full_gated = lax.all_gather(gated, 'chan', axis=0)]
    ppermute x0 -> x4, waiting for transfers between devices: none -> 6.19 us  [the longest x3 5.3 us: local(): pairs.append(lax.ppermute(pair, 'chan', route))]
    ppermute x0 -> x4, starting transfers between devices: none -> 3.62 us  [the longest x3 3.09 us: local(): pairs.append(lax.ppermute(pair, 'chan', route))]
    all_to_all x1, waiting for transfers between devices: 3.1 us -> 6.59 us  [local(): lax.all_to_all(weight_part, 'ctx', 0, 0, axis_index_groups=along_z)]
    all_to_all x1, blocking collectives: 24.8 us -> 23.2 us  [local(): lax.all_to_all(sent.reshape(32, 40, 128), 'ctx', 0, 0).reshape(1280, 128)]
  transfers between devices with their start and end apart: 5 -> 9, of which waited for: 1 -> 5; matrix products, arithmetic and copies ran while one was open for 0% -> 0% of each run, Pallas kernels for 7% -> 7%
where the time goes in v4:
time: 114 us; the launch traced here: 113 us
  blocking collectives  70.1 us (61%)
  Pallas kernels  15.3 us (13%)
  starting transfers between devices  13.5 us (12%)
  waiting for transfers between devices  12.8 us (11%)
    all_to_all x1, blocking collectives, local(): lax.all_to_all(sent.reshape(32, 40, 128), 'ctx', 0, 0).reshape(1280, 128)  23.2 us
    all_to_all x1, blocking collectives, local(): lax.all_to_all(plane_sent, ('ctx', 'chan'), 0, 0, axis_index_groups=planes)  18.8 us
    all_to_all x1, blocking collectives, local(): lax.all_to_all(convolved.reshape(32, 16, 128), 'ctx', 0, 0)  14.1 us
    all_to_all x1, blocking collectives, local(): partials = lax.all_to_all(partials, 'chan', 0, 0)  14 us
    all_to_all x1, waiting for transfers between devices, local(): lax.all_to_all(weight_part, 'ctx', 0, 0, axis_index_groups=along_z)  6.59 us
    pallas_call x1, Pallas kernels, conv_call(): pl.pallas_call(conv_kernel, out_shape=jax.ShapeDtypeStruct((512, 128), f3...  6.41 us
    ppermute x3, waiting for transfers between devices, local(): pairs.append(lax.ppermute(pair, 'chan', route))  5.3 us
    pallas_call x1, Pallas kernels, partial_call(): pl.pallas_call(partial_kernel, out_shape=jax.ShapeDtypeStruct((8, 224, 12...  4.17 us
  transfers between devices with their start and end apart: 9, of which 5 were waited for; matrix products, arithmetic and copies ran while one was open for 0% of the time, Pallas kernels for 7%

profile of v4, /device:TPU:1, one launch (start us, length us, event | category | flops | bytes accessed | tf_op | source)
XLA Modules:
  0.0 113.4 jit_solution(7753270780771047182)
XLA Ops:
  0.7 4.2 %shard_map.101 = bf16[8,224,128]{2,1,0:T(8,128)(2,1)} custom-call(bf16[224,1024]{1,0:T(8,128)(2,1)} %own.1, bf16[1024,1024]{1,0:T(8,128)(2,1)} %weight_ref.1), custom_call_target="tpu_custom_call" | custom-call | tf_op jit(solution)/shard_map/pallas_call | solution.py:52
  4.9 3.6 %collective-permute-start.1 = (bf16[224,1024]{1,0:T(8,128)(2,1)S(1)}, bf16[224,1024]{1,0:T(8,128)(2,1)S(1)}, u32[]{:S(2)}, u32[]{:S(2)}) collective-permute-start(bf16[224,1024]{1,0:T(8,128)(2,1)S(1)} %copy-done.1), channel_id=1, source_target_pairs={{0,24},{8,0},{16,8},{24,16},{32,56},{40,32},{48,40},{56,48},{64,88... | collective-permute-start | bytes 1376264 | tf_op jit(solution)/shard_map/ppermute | solution.py:362
  8.5 14.0 %all_to_all.25.partial_ref = bf16[8,224,128]{2,1,0:T(8,128)(2,1)S(1)} all-to-all(bf16[8,224,128]{2,1,0:T(8,128)(2,1)} %shard_map.101), channel_id=1, replica_groups=mesh['ctx'=32,'chan'=8] {'chan'}, dimensions={0} | all-to-all | bytes 917504 | tf_op jit(solution)/shard_map/all_to_all | solution.py:360
  22.5 0.2 shard_map.102
  22.8 23.2 %all_to_all.26 = bf16[32,40,128]{2,1,0:T(8,128)(2,1)S(1)} all-to-all(bf16[32,40,128]{2,1,0:T(8,128)(2,1)S(1)} %bitcast.12), channel_id=1, replica_groups=mesh['ctx'=32,'chan'=8] {'ctx'}, dimensions={0} | all-to-all | bytes 655360 | tf_op jit(solution)/shard_map/all_to_all | solution.py:365
  46.0 0.5 collective-permute-start.3
  46.5 2.2 %collective-permute-start.2 = (bf16[112,1024]{1,0:T(8,128)(2,1)S(1)}, bf16[112,1024]{1,0:T(8,128)(2,1)S(1)}, u32[]{:S(2)}, u32[]{:S(2)}) collective-permute-start(bf16[112,1024]{1,0:T(8,128)(2,1)S(1)} %slice.6), channel_id=1, source_target_pairs={{0,24},{8,0},{16,8},{24,16},{32,56},{40,32},{48,40},{56,48},{64,88... | collective-permute-start | bytes 688136 | tf_op jit(solution)/shard_map/ppermute | solution.py:367
  48.8 6.4 %shard_map.103 = f32[512,128]{1,0:T(8,128)S(1)} custom-call(bf16[1280,128]{1,0:T(8,128)(2,1)S(1)} %bitcast.9), custom_call_target="tpu_custom_call" | custom-call | tf_op jit(solution)/shard_map/pallas_call | solution.py:187
  55.2 14.1 %all_to_all.27 = f32[32,16,128]{2,1,0:T(8,128)S(1)} all-to-all(f32[32,16,128]{2,1,0:T(8,128)S(1)} %bitcast.10), channel_id=1, replica_groups=mesh['ctx'=32,'chan'=8] {'ctx'}, dimensions={0} | all-to-all | bytes 524288 | tf_op jit(solution)/shard_map/all_to_all | solution.py:371
  69.4 1.0 shard_map.104
  70.4 18.8 %all_to_all.28.gated_ref = bf16[32,64,128]{2,1,0:T(8,128)(2,1)S(1)} all-to-all(bf16[32,64,128]{2,1,0:T(8,128)(2,1)S(1)} %get-tuple-element.41), channel_id=1, replica_groups={{0,1,2,3,4,5,6,7,8,9,10,11,12,13,14,15,16,17,18,19,20,21,22,23,24,25,26..., dimensions={0} | all-to-all | bytes 1048576 | tf_op jit(solution)/shard_map/all_to_all | solution.py:375
  89.2 2.0 %shard_map.105 = bf16[256,1024]{1,0:T(8,128)(2,1)} custom-call(s32[1]{0:T(128)} %bitcast.own_ref, bf16[32,64,128]{2,1,0:T(8,128)(2,1)S(1)} %all_to_all.28.gated_ref, bf16[224,1024]{1,0:T(8,128)(2,1)S(1)} %copy-done.1, bf16[224,1024]{1,0:T(8,128)(2,1)S(1)} %collective-permute-done.before, bf16[224,1024]{1,0:T(8,128)(2,1)S(1)} %collective-permute-done.1.after, ...), custom_call_target="tpu_custom_call" | custom-call | flops 469762048 | bytes 3145728 | tf_op jit(solution)/shard_map/pallas_call | solution.py:298
  91.3 3.5 %all-to-all-start.4 = ((bf16[8,32,1024]{2,1,0:T(8,128)(2,1)}), bf16[8,32,1024]{2,1,0:T(8,128)(2,1)S(1)}, u32[]{:S(2)}, u32[]{:S(2)}) async-start(bf16[8,32,1024]{2,1,0:T(8,128)(2,1)} %bitcast.6), calls=%async_computation.4 | async-start | bytes 1048576 | tf_op jit(solution)/shard_map/all_to_all | solution.py:380
  94.8 0.5 collective-permute-start.4
  95.3 0.9 collective-permute-done.4
  96.2 0.5 collective-permute-start.7
  96.8 1.9 %collective-permute-start.6 = (bf16[2,224,128]{2,1,0:T(8,128)(2,1)S(1)}, bf16[2,224,128]{2,1,0:T(8,128)(2,1)S(1)}, u32[]{:S(2)}, u32[]{:S(2)}) collective-permute-start(bf16[2,224,128]{2,1,0:T(8,128)(2,1)S(1)} %pad_maximum_fusion.pair_0), channel_id=1, source_target_pairs={{4,0},{5,1},{6,2},{7,3},{0,4},{1,5},{2,6},{3,7},{12,8},{13,9},{14,... | collective-permute-start | bytes 344072 | tf_op jit(solution)/shard_map/ppermute | solution.py:386
  98.7 0.6 collective-permute-start.5
  99.3 2.6 %collective-permute-done.7.pair_3 = bf16[2,224,128]{2,1,0:T(8,128)(2,1)S(1)} collective-permute-done((bf16[2,224,128]{2,1,0:T(8,128)(2,1)S(1)}, bf16[2,224,128]{2,1,0:T(8,128)(2,1)S(1)}, u32[]{:S(2)}, u32[]{:S(2)}) %collective-permute-start.7) | collective-permute-done | bytes 114720 | tf_op jit(solution)/shard_map/ppermute | solution.py:386
  102.0 2.4 %collective-permute-done.6.pair_2 = bf16[2,224,128]{2,1,0:T(8,128)(2,1)S(1)} collective-permute-done((bf16[2,224,128]{2,1,0:T(8,128)(2,1)S(1)}, bf16[2,224,128]{2,1,0:T(8,128)(2,1)S(1)}, u32[]{:S(2)}, u32[]{:S(2)}) %collective-permute-start.6) | collective-permute-done | bytes 114720 | tf_op jit(solution)/shard_map/ppermute | solution.py:386
  104.3 0.3 collective-permute-done.5.pair_1
  104.6 1.4 %shard_map.106 = f32[224,1024]{1,0:T(8,128)} custom-call(s32[1]{0:T(128)} %bitcast.1.own_ref, bf16[2,224,128]{2,1,0:T(8,128)(2,1)S(1)} %pad_maximum_fusion.pair_0, bf16[2,224,128]{2,1,0:T(8,128)(2,1)S(1)} %collective-permute-done.5.pair_1, bf16[2,224,128]{2,1,0:T(8,128)(2,1)S(1)} %collective-permute-done.6.pair_2, ...), custom_call_target="tpu_custom_call" | custom-call | tf_op jit(solution)/shard_map/pallas_call | solution.py:337
  106.1 6.6 %all-to-all-done.4 = bf16[8,32,1024]{2,1,0:T(8,128)(2,1)S(1)} async-done(((bf16[8,32,1024]{2,1,0:T(8,128)(2,1)}), bf16[8,32,1024]{2,1,0:T(8,128)(2,1)S(1)}, u32[]{:S(2)}, u32[]{:S(2)}) %all-to-all-start.4) | async-done | bytes 524320 | tf_op jit(solution)/shard_map/all_to_all | solution.py:380
  112.7 0.7 convert_reduce_fusion
  (20 shorter events, 0.1 us)
Async XLA Ops:
  0.6 4.2 %copy-start.1 = (bf16[224,1024]{1,0:T(8,128)(2,1)S(1)}, bf16[224,1024]{1,0:T(8,128)(2,1)}, u32[]{:S(2)}) copy-start(bf16[224,1024]{1,0:T(8,128)(2,1)} %own.1) | copy-start | bytes 1376260
  0.6 21.9 %copy-start.4 = (bf16[224,128]{1,0:T(8,128)(2,1)S(1)}, bf16[224,128]{1,0:T(8,128)(2,1)}, u32[]{:S(2)}) copy-start(bf16[224,128]{1,0:T(8,128)(2,1)} %value_ref.3) | copy-start | bytes 172036
  0.7 21.9 %copy-start.3 = (bf16[224,128]{1,0:T(8,128)(2,1)S(1)}, bf16[224,128]{1,0:T(8,128)(2,1)}, u32[]{:S(2)}) copy-start(bf16[224,128]{1,0:T(8,128)(2,1)} %key_ref.3) | copy-start | bytes 172036
  0.7 21.9 %copy-start.2 = (bf16[224,128]{1,0:T(8,128)(2,1)S(1)}, bf16[224,128]{1,0:T(8,128)(2,1)}, u32[]{:S(2)}) copy-start(bf16[224,128]{1,0:T(8,128)(2,1)} %query_ref.3) | copy-start | bytes 172036
  0.7 21.9 %copy-start.5 = (f32[224,128]{1,0:T(8,128)S(1)}, f32[224,128]{1,0:T(8,128)}, u32[]{:S(2)}) copy-start(f32[224,128]{1,0:T(8,128)} %filter_ref.1) | copy-start | bytes 344068
  4.9 17.9 %collective-permute-start.1 = (bf16[224,1024]{1,0:T(8,128)(2,1)S(1)}, bf16[224,1024]{1,0:T(8,128)(2,1)S(1)}, u32[]{:S(2)}, u32[]{:S(2)}) collective-permute-start(bf16[224,1024]{1,0:T(8,128)(2,1)S(1)} %copy-done.1), channel_id=1, source_target_pairs={{0,24},{8,0},{16,8},{24,16},{32,56},{40,32},{48,40},{56,48},{64,88... | collective-permute-start | bytes 1376264 | tf_op jit(solution)/shard_map/ppermute | solution.py:362
  8.5 14.3 %collective-permute-start = (bf16[224,1024]{1,0:T(8,128)(2,1)S(1)}, bf16[224,1024]{1,0:T(8,128)(2,1)S(1)}, u32[]{:S(2)}, u32[]{:S(2)}) collective-permute-start(bf16[224,1024]{1,0:T(8,128)(2,1)S(1)} %copy-done.1), channel_id=1, source_target_pairs={{0,8},{8,16},{16,24},{24,0},{32,40},{40,48},{48,56},{56,32},{64,72... | collective-permute-start | bytes 1376264 | tf_op jit(solution)/shard_map/ppermute | solution.py:361
  46.0 9.2 %collective-permute-start.3 = (bf16[112,1024]{1,0:T(8,128)(2,1)S(1)}, bf16[112,1024]{1,0:T(8,128)(2,1)S(1)}, u32[]{:S(2)}, u32[]{:S(2)}) collective-permute-start(bf16[112,1024]{1,0:T(8,128)(2,1)S(1)} %slice.7), channel_id=1, source_target_pairs={{0,8},{8,16},{16,24},{24,0},{32,40},{40,48},{48,56},{56,32},{64,72... | collective-permute-start | bytes 688136 | tf_op jit(solution)/shard_map/ppermute | solution.py:368
  46.5 8.7 %collective-permute-start.2 = (bf16[112,1024]{1,0:T(8,128)(2,1)S(1)}, bf16[112,1024]{1,0:T(8,128)(2,1)S(1)}, u32[]{:S(2)}, u32[]{:S(2)}) collective-permute-start(bf16[112,1024]{1,0:T(8,128)(2,1)S(1)} %slice.6), channel_id=1, source_target_pairs={{0,24},{8,0},{16,8},{24,16},{32,56},{40,32},{48,40},{56,48},{64,88... | collective-permute-start | bytes 688136 | tf_op jit(solution)/shard_map/ppermute | solution.py:367
  89.2 15.4 %copy-start = (bf16[1024,1024]{1,0:T(8,128)(2,1)S(1)}, bf16[1024,1024]{1,0:T(8,128)(2,1)}, u32[]{:S(2)}) copy-start(bf16[1024,1024]{1,0:T(8,128)(2,1)} %weight_ref.1) | copy-start | bytes 6291460
  91.3 21.4 %all-to-all-start.4 = ((bf16[8,32,1024]{2,1,0:T(8,128)(2,1)}), bf16[8,32,1024]{2,1,0:T(8,128)(2,1)S(1)}, u32[]{:S(2)}, u32[]{:S(2)}) async-start(bf16[8,32,1024]{2,1,0:T(8,128)(2,1)} %bitcast.6), calls=%async_computation.4 | async-start | bytes 1048576 | tf_op jit(solution)/shard_map/all_to_all | solution.py:380
  94.8 1.4 %collective-permute-start.4 = (bf16[224,128]{1,0:T(8,128)(2,1)S(1)}, bf16[224,128]{1,0:T(8,128)(2,1)S(1)}, u32[]{:S(2)}, u32[]{:S(2)}) collective-permute-start(bf16[224,128]{1,0:T(8,128)(2,1)S(1)} %get-tuple-element.44), channel_id=1, source_target_pairs={{0,1},{1,0},{2,3},{3,2},{4,5},{5,4},{6,7},{7,6},{8,9},{9,8},{10,11... | collective-permute-start | bytes 172040 | tf_op jit(solution)/shard_map/ppermute | solution.py:381
  96.2 5.7 %collective-permute-start.7 = (bf16[2,224,128]{2,1,0:T(8,128)(2,1)S(1)}, bf16[2,224,128]{2,1,0:T(8,128)(2,1)S(1)}, u32[]{:S(2)}, u32[]{:S(2)}) collective-permute-start(bf16[2,224,128]{2,1,0:T(8,128)(2,1)S(1)} %pad_maximum_fusion.pair_0), channel_id=1, source_target_pairs={{6,0},{7,1},{0,2},{1,3},{2,4},{3,5},{4,6},{5,7},{14,8},{15,9},{8,1... | collective-permute-start | bytes 344072 | tf_op jit(solution)/shard_map/ppermute | solution.py:386
  96.8 7.6 %collective-permute-start.6 = (bf16[2,224,128]{2,1,0:T(8,128)(2,1)S(1)}, bf16[2,224,128]{2,1,0:T(8,128)(2,1)S(1)}, u32[]{:S(2)}, u32[]{:S(2)}) collective-permute-start(bf16[2,224,128]{2,1,0:T(8,128)(2,1)S(1)} %pad_maximum_fusion.pair_0), channel_id=1, source_target_pairs={{4,0},{5,1},{6,2},{7,3},{0,4},{1,5},{2,6},{3,7},{12,8},{13,9},{14,... | collective-permute-start | bytes 344072 | tf_op jit(solution)/shard_map/ppermute | solution.py:386
  98.7 5.9 %collective-permute-start.5 = (bf16[2,224,128]{2,1,0:T(8,128)(2,1)S(1)}, bf16[2,224,128]{2,1,0:T(8,128)(2,1)S(1)}, u32[]{:S(2)}, u32[]{:S(2)}) collective-permute-start(bf16[2,224,128]{2,1,0:T(8,128)(2,1)S(1)} %pad_maximum_fusion.pair_0), channel_id=1, source_target_pairs={{2,0},{3,1},{4,2},{5,3},{6,4},{7,5},{0,6},{1,7},{10,8},{11,9},{12,... | collective-permute-start | bytes 344072 | tf_op jit(solution)/shard_map/ppermute | solution.py:386

commit v5 on v4

--- a/solution.py
+++ b/solution.py
@@ -202,62 +202,72 @@
     )(recv)
 
 
-def unpack_kernel(
-    recv_ref, query_ref, key_ref, value_ref, grad_ref, send_ref, gated_hbm, gq_ref, gk_ref, gv_ref,
-    gated_ref, sem,
-):
+def by_token_block(recv_ref, index, half):
+    pieces = [recv_ref[pl.ds((index * 2 + half) * 4 + cc, 32, stride=16), :] for cc in range(4)]
+    return jnp.concatenate(pieces, axis=0)
+
+
+def gate_kernel(recv_ref, query_ref, send_ref, gated_ref, conv_ref):
     f32 = jnp.float32
     pad = jnp.zeros((16, 128), f32)
-    gated_copies = []
     for half in range(2):
         rows = slice(112 * half, 112 * half + 112)
-        blocks = []
-        for index in range(2):
-            pieces = [recv_ref[pl.ds((index * 2 + half) * 4 + cc, 32, stride=16), :] for cc in range(4)]
-            blocks.append(jnp.concatenate(pieces, axis=0))
-        conv_out = blocks[0].T[0:112]
-        grad_mixed = blocks[1].T[0:112]
+        block = by_token_block(recv_ref, 0, half)
         query = query_ref[rows, :].astype(f32)
-        by_channel = jnp.concatenate([query, pad], axis=0).T * blocks[0]
+        by_channel = jnp.concatenate([query, pad], axis=0).T * block
         by_channel = by_channel.astype(jnp.bfloat16)
         for y in range(4):
             for j in range(8):
                 send_ref[8 * y + j, 32 * half:32 * half + 32, :] = by_channel[32 * y:32 * y + 32]
+        conv_out = block.T[0:112]
+        conv_ref[rows, :] = conv_out
         gated_ref[rows, :] = (query * conv_out).astype(jnp.bfloat16)
-        gq_ref[rows, :] = grad_ref[rows, :] * conv_out
-        gated_copy = pltpu.make_async_copy(
-            gated_ref.at[pl.ds(112 * half, 112)], gated_hbm.at[pl.ds(112 * half, 112)], sem.at[half]
-        )
-        gated_copy.start()
-        gated_copies.append(gated_copy)
-        gk_ref[rows, :] = grad_mixed * value_ref[rows, :].astype(f32)
-        gv_ref[rows, :] = grad_mixed * key_ref[rows, :].astype(f32)
-    for gated_copy in gated_copies:
-        gated_copy.wait()
-
-
-def unpack_call(recv, query, key, value, grad_gated):
+
+
+def gate_call(recv, query):
     bf = jnp.bfloat16
-    grad = jax.ShapeDtypeStruct((224, 128), jnp.float32)
-    return pl.pallas_call(
-        unpack_kernel,
+    return pl.pallas_call(
+        gate_kernel,
         out_shape=(
             jax.ShapeDtypeStruct((32, 64, 128), bf),
             jax.ShapeDtypeStruct((224, 128), bf),
-            grad,
-            grad,
-            grad,
+            jax.ShapeDtypeStruct((224, 128), jnp.float32),
         ),
-        out_specs=tuple(
-            pl.BlockSpec(memory_space=pltpu.MemorySpace.HBM if index == 1 else pltpu.VMEM)
-            for index in range(5)
-        ),
-        scratch_shapes=[
-            pltpu.VMEM((224, 128), bf),
-            pltpu.SemaphoreType.DMA((2,)),
-        ],
         compiler_params=pltpu.CompilerParams(vmem_limit_bytes=VMEM_BYTES),
-    )(recv, query, key, value, grad_gated)
+    )(recv, query)
+
+
+def grads_kernel(recv_ref, conv_ref, key_ref, value_ref, grad_ref, gq_ref, gk_ref, gv_ref):
+    f32 = jnp.float32
+    gq_ref[...] = grad_ref[...] * conv_ref[...]
+    for half in range(2):
+        rows = slice(112 * half, 112 * half + 112)
+        grad_mixed = by_token_block(recv_ref, 1, half).T[0:112]
+        gk_ref[rows, :] = grad_mixed * value_ref[rows, :].astype(f32)
+        gv_ref[rows, :] = grad_mixed * key_ref[rows, :].astype(f32)
+
+
+def grads_call(recv, conv_out, key, value, grad_gated):
+    return pl.pallas_call(
+        grads_kernel,
+        out_shape=(jax.ShapeDtypeStruct((224, 128), jnp.float32),) * 3,
+        compiler_params=pltpu.CompilerParams(vmem_limit_bytes=4 * 1024 * 1024),
+    )(recv, conv_out, key, value, grad_gated)
+
+
+def sum_kernel(parts_ref, out_ref):
+    total = parts_ref[0].astype(jnp.float32)
+    for index in range(1, 8):
+        total = total + parts_ref[index].astype(jnp.float32)
+    out_ref[...] = total
+
+
+def sum_call(parts):
+    return pl.pallas_call(
+        sum_kernel,
+        out_shape=jax.ShapeDtypeStruct((32, 1024), jnp.float32),
+        compiler_params=pltpu.CompilerParams(vmem_limit_bytes=4 * 1024 * 1024),
+    )(parts)
 
 
 def weight_kernel(own_ref, gated_ref, own, before, after, far_low, far_high, out_hbm, out_ref, sem):
@@ -369,14 +379,12 @@
     convolved = conv_call(by_channel)
     far_low, far_high, convolved = together((far_low, far_high, convolved))
     by_token = lax.all_to_all(convolved.reshape(32, 16, 128), "ctx", 0, 0).reshape(512, 128)
-    plane_sent, gated, grad_query, grad_key, grad_value = unpack_call(
-        by_token, query_slab, key_slab, value_slab, grad_gated
-    )
+    plane_sent, gated, conv_out = gate_call(by_token, query_slab)
     plane_gated = lax.all_to_all(plane_sent, ("ctx", "chan"), 0, 0, axis_index_groups=planes)
     weight_part = weight_call(
         own_y, plane_gated, (grad_out, before, after, far_low, far_high)
     ).reshape(8, 32, 1024)
-    gated, weight_part = together((gated, weight_part))
+    gated, conv_out, weight_part = together((gated, conv_out, weight_part))
     arrived = lax.all_to_all(weight_part, "ctx", 0, 0, axis_index_groups=along_z)
     other = lax.ppermute(gated, "chan", [(i, i ^ 1) for i in range(8)])
     pair = jnp.stack([gated, other])
@@ -385,7 +393,10 @@
         route = [((i + 2 * turn) % 8, i) for i in range(8)]
         pairs.append(lax.ppermute(pair, "chan", route))
     layer_out = layer_call(own_chan, pairs, out_weight)
-    grad_weight = jnp.sum(arrived.astype(jnp.float32), axis=0)
+    grad_query, grad_key, grad_value = grads_call(
+        by_token, conv_out, key_slab, value_slab, grad_gated
+    )
+    grad_weight = sum_call(arrived)
     return (layer_out, grad_query, grad_key, grad_value, grad_weight)
 
 

time: 114 us -> 113 us (level)
  transfers between devices with their start and end apart: 9 -> 9, of which waited for: 5 -> 5; matrix products, arithmetic and copies ran while one was open for 0% -> 0% of each run, Pallas kernels for 7% -> 8%
where the time goes in v5:
time: 113 us; the launch traced here: 112 us
  blocking collectives  70.1 us (62%)
  Pallas kernels  16 us (14%)
  starting transfers between devices  13.5 us (12%)
  waiting for transfers between devices  12 us (11%)
    all_to_all x1, blocking collectives, local(): lax.all_to_all(sent.reshape(32, 40, 128), 'ctx', 0, 0).reshape(1280, 128)  23.2 us
    all_to_all x1, blocking collectives, local(): lax.all_to_all(plane_sent, ('ctx', 'chan'), 0, 0, axis_index_groups=planes)  18.8 us
    all_to_all x1, blocking collectives, local(): lax.all_to_all(convolved.reshape(32, 16, 128), 'ctx', 0, 0)  14.1 us
    all_to_all x1, blocking collectives, local(): partials = lax.all_to_all(partials, 'chan', 0, 0)  14 us
    all_to_all x1, waiting for transfers between devices, local(): lax.all_to_all(weight_part, 'ctx', 0, 0, axis_index_groups=along_z)  6.59 us
    pallas_call x1, Pallas kernels, conv_call(): pl.pallas_call(conv_kernel, out_shape=jax.ShapeDtypeStruct((512, 128), f3...  6.41 us
    ppermute x3, waiting for transfers between devices, local(): pairs.append(lax.ppermute(pair, 'chan', route))  4.51 us
    pallas_call x1, Pallas kernels, partial_call(): pl.pallas_call(partial_kernel, out_shape=jax.ShapeDtypeStruct((8, 224, 12...  4.17 us
  transfers between devices with their start and end apart: 9, of which 5 were waited for; matrix products, arithmetic and copies ran while one was open for 0% of the time, Pallas kernels for 8%

profile of v5, /device:TPU:1, one launch (start us, length us, event | category | flops | bytes accessed | tf_op | source)
XLA Modules:
  0.0 112.5 jit_solution(17309097763365519609)
XLA Ops:
  0.7 4.2 %shard_map.101 = bf16[8,224,128]{2,1,0:T(8,128)(2,1)} custom-call(bf16[224,1024]{1,0:T(8,128)(2,1)} %own.1, bf16[1024,1024]{1,0:T(8,128)(2,1)} %weight_ref.1), custom_call_target="tpu_custom_call" | custom-call | tf_op jit(solution)/shard_map/pallas_call | solution.py:52
  4.9 3.6 %collective-permute-start.1 = (bf16[224,1024]{1,0:T(8,128)(2,1)S(1)}, bf16[224,1024]{1,0:T(8,128)(2,1)S(1)}, u32[]{:S(2)}, u32[]{:S(2)}) collective-permute-start(bf16[224,1024]{1,0:T(8,128)(2,1)S(1)} %copy-done.1), channel_id=1, source_target_pairs={{0,24},{8,0},{16,8},{24,16},{32,56},{40,32},{48,40},{56,48},{64,88... | collective-permute-start | bytes 1376264 | tf_op jit(solution)/shard_map/ppermute | solution.py:372
  8.5 14.0 %all_to_all.25.partial_ref = bf16[8,224,128]{2,1,0:T(8,128)(2,1)S(1)} all-to-all(bf16[8,224,128]{2,1,0:T(8,128)(2,1)} %shard_map.101), channel_id=1, replica_groups=mesh['ctx'=32,'chan'=8] {'chan'}, dimensions={0} | all-to-all | bytes 917504 | tf_op jit(solution)/shard_map/all_to_all | solution.py:370
  22.5 0.2 shard_map.102
  22.8 23.2 %all_to_all.26 = bf16[32,40,128]{2,1,0:T(8,128)(2,1)S(1)} all-to-all(bf16[32,40,128]{2,1,0:T(8,128)(2,1)S(1)} %bitcast.13), channel_id=1, replica_groups=mesh['ctx'=32,'chan'=8] {'ctx'}, dimensions={0} | all-to-all | bytes 655360 | tf_op jit(solution)/shard_map/all_to_all | solution.py:375
  46.0 0.5 collective-permute-start.3
  46.5 2.2 %collective-permute-start.2 = (bf16[112,1024]{1,0:T(8,128)(2,1)S(1)}, bf16[112,1024]{1,0:T(8,128)(2,1)S(1)}, u32[]{:S(2)}, u32[]{:S(2)}) collective-permute-start(bf16[112,1024]{1,0:T(8,128)(2,1)S(1)} %slice.6), channel_id=1, source_target_pairs={{0,24},{8,0},{16,8},{24,16},{32,56},{40,32},{48,40},{56,48},{64,88... | collective-permute-start | bytes 688136 | tf_op jit(solution)/shard_map/ppermute | solution.py:377
  48.8 6.4 %shard_map.103 = f32[512,128]{1,0:T(8,128)S(1)} custom-call(bf16[1280,128]{1,0:T(8,128)(2,1)S(1)} %bitcast.11), custom_call_target="tpu_custom_call" | custom-call | tf_op jit(solution)/shard_map/pallas_call | solution.py:187
  55.2 14.1 %all_to_all.27 = f32[32,16,128]{2,1,0:T(8,128)S(1)} all-to-all(f32[32,16,128]{2,1,0:T(8,128)S(1)} %bitcast.12), channel_id=1, replica_groups=mesh['ctx'=32,'chan'=8] {'ctx'}, dimensions={0} | all-to-all | bytes 524288 | tf_op jit(solution)/shard_map/all_to_all | solution.py:381
  69.5 18.8 %all_to_all.28.gated_ref = bf16[32,64,128]{2,1,0:T(8,128)(2,1)S(1)} all-to-all(bf16[32,64,128]{2,1,0:T(8,128)(2,1)S(1)} %get-tuple-element.43), channel_id=1, replica_groups={{0,1,2,3,4,5,6,7,8,9,10,11,12,13,14,15,16,17,18,19,20,21,22,23,24,25,26..., dimensions={0} | all-to-all | bytes 1048576 | tf_op jit(solution)/shard_map/all_to_all | solution.py:383
  88.3 2.0 %shard_map.105 = bf16[256,1024]{1,0:T(8,128)(2,1)} custom-call(s32[1]{0:T(128)} %bitcast.own_ref, bf16[32,64,128]{2,1,0:T(8,128)(2,1)S(1)} %all_to_all.28.gated_ref, bf16[224,1024]{1,0:T(8,128)(2,1)S(1)} %copy-done.1, bf16[224,1024]{1,0:T(8,128)(2,1)S(1)} %collective-permute-done.before, bf16[224,1024]{1,0:T(8,128)(2,1)S(1)} %collective-permute-done.1.after, ...), custom_call_target="tpu_custom_call" | custom-call | flops 469762048 | bytes 3145728 | tf_op jit(solution)/shard_map/pallas_call | solution.py:308
  90.4 3.5 %all-to-all-start.4 = ((bf16[8,32,1024]{2,1,0:T(8,128)(2,1)}), bf16[8,32,1024]{2,1,0:T(8,128)(2,1)S(1)}, u32[]{:S(2)}, u32[]{:S(2)}) async-start(bf16[8,32,1024]{2,1,0:T(8,128)(2,1)} %bitcast.6), calls=%async_computation.4 | async-start | bytes 1048576 | tf_op jit(solution)/shard_map/all_to_all | solution.py:388
  93.9 0.5 collective-permute-start.4
  94.4 0.9 collective-permute-done.4
  95.3 0.5 collective-permute-start.7
  95.9 1.9 %collective-permute-start.6 = (bf16[2,224,128]{2,1,0:T(8,128)(2,1)S(1)}, bf16[2,224,128]{2,1,0:T(8,128)(2,1)S(1)}, u32[]{:S(2)}, u32[]{:S(2)}) collective-permute-start(bf16[2,224,128]{2,1,0:T(8,128)(2,1)S(1)} %pad_maximum_fusion.pair_0), channel_id=1, source_target_pairs={{4,0},{5,1},{6,2},{7,3},{0,4},{1,5},{2,6},{3,7},{12,8},{13,9},{14,... | collective-permute-start | bytes 344072 | tf_op jit(solution)/shard_map/ppermute | solution.py:394
  97.8 0.6 collective-permute-start.5
  98.4 0.8 shard_map.107
  99.2 1.9 %collective-permute-done.7.pair_3 = bf16[2,224,128]{2,1,0:T(8,128)(2,1)S(1)} collective-permute-done((bf16[2,224,128]{2,1,0:T(8,128)(2,1)S(1)}, bf16[2,224,128]{2,1,0:T(8,128)(2,1)S(1)}, u32[]{:S(2)}, u32[]{:S(2)}) %collective-permute-start.7) | collective-permute-done | bytes 114720 | tf_op jit(solution)/shard_map/ppermute | solution.py:394
  101.1 2.4 %collective-permute-done.6.pair_2 = bf16[2,224,128]{2,1,0:T(8,128)(2,1)S(1)} collective-permute-done((bf16[2,224,128]{2,1,0:T(8,128)(2,1)S(1)}, bf16[2,224,128]{2,1,0:T(8,128)(2,1)S(1)}, u32[]{:S(2)}, u32[]{:S(2)}) %collective-permute-start.6) | collective-permute-done | bytes 114720 | tf_op jit(solution)/shard_map/ppermute | solution.py:394
  103.4 0.3 collective-permute-done.5.pair_1
  103.7 1.5 %shard_map.106 = f32[224,1024]{1,0:T(8,128)} custom-call(s32[1]{0:T(128)} %bitcast.1.own_ref, bf16[2,224,128]{2,1,0:T(8,128)(2,1)S(1)} %pad_maximum_fusion.pair_0, bf16[2,224,128]{2,1,0:T(8,128)(2,1)S(1)} %collective-permute-done.5.pair_1, bf16[2,224,128]{2,1,0:T(8,128)(2,1)S(1)} %collective-permute-done.6.pair_2, ...), custom_call_target="tpu_custom_call" | custom-call | tf_op jit(solution)/shard_map/pallas_call | solution.py:347
  105.2 6.6 %all-to-all-done.4.parts_ref = bf16[8,32,1024]{2,1,0:T(8,128)(2,1)S(1)} async-done(((bf16[8,32,1024]{2,1,0:T(8,128)(2,1)}), bf16[8,32,1024]{2,1,0:T(8,128)(2,1)S(1)}, u32[]{:S(2)}, u32[]{:S(2)}) %all-to-all-start.4) | async-done | bytes 524320 | tf_op jit(solution)/shard_map/all_to_all | solution.py:388
  111.8 0.7 shard_map.108
  (21 shorter events, 0.2 us)
Async XLA Ops:
  0.6 4.2 %copy-start.1 = (bf16[224,1024]{1,0:T(8,128)(2,1)S(1)}, bf16[224,1024]{1,0:T(8,128)(2,1)}, u32[]{:S(2)}) copy-start(bf16[224,1024]{1,0:T(8,128)(2,1)} %own.1) | copy-start | bytes 1376260
  0.6 21.9 %copy-start.3 = (bf16[224,128]{1,0:T(8,128)(2,1)S(1)}, bf16[224,128]{1,0:T(8,128)(2,1)}, u32[]{:S(2)}) copy-start(bf16[224,128]{1,0:T(8,128)(2,1)} %value_ref.3) | copy-start | bytes 172036
  0.7 21.9 %copy-start.2 = (bf16[224,128]{1,0:T(8,128)(2,1)S(1)}, bf16[224,128]{1,0:T(8,128)(2,1)}, u32[]{:S(2)}) copy-start(bf16[224,128]{1,0:T(8,128)(2,1)} %key_ref.3) | copy-start | bytes 172036
  0.7 21.9 %copy-start.4 = (bf16[224,128]{1,0:T(8,128)(2,1)S(1)}, bf16[224,128]{1,0:T(8,128)(2,1)}, u32[]{:S(2)}) copy-start(bf16[224,128]{1,0:T(8,128)(2,1)} %query_ref.3) | copy-start | bytes 172036
  0.7 21.9 %copy-start.5 = (f32[224,128]{1,0:T(8,128)S(1)}, f32[224,128]{1,0:T(8,128)}, u32[]{:S(2)}) copy-start(f32[224,128]{1,0:T(8,128)} %filter_ref.1) | copy-start | bytes 344068
  4.9 17.9 %collective-permute-start.1 = (bf16[224,1024]{1,0:T(8,128)(2,1)S(1)}, bf16[224,1024]{1,0:T(8,128)(2,1)S(1)}, u32[]{:S(2)}, u32[]{:S(2)}) collective-permute-start(bf16[224,1024]{1,0:T(8,128)(2,1)S(1)} %copy-done.1), channel_id=1, source_target_pairs={{0,24},{8,0},{16,8},{24,16},{32,56},{40,32},{48,40},{56,48},{64,88... | collective-permute-start | bytes 1376264 | tf_op jit(solution)/shard_map/ppermute | solution.py:372
  8.5 14.3 %collective-permute-start = (bf16[224,1024]{1,0:T(8,128)(2,1)S(1)}, bf16[224,1024]{1,0:T(8,128)(2,1)S(1)}, u32[]{:S(2)}, u32[]{:S(2)}) collective-permute-start(bf16[224,1024]{1,0:T(8,128)(2,1)S(1)} %copy-done.1), channel_id=1, source_target_pairs={{0,8},{8,16},{16,24},{24,0},{32,40},{40,48},{48,56},{56,32},{64,72... | collective-permute-start | bytes 1376264 | tf_op jit(solution)/shard_map/ppermute | solution.py:371
  46.0 9.2 %collective-permute-start.3 = (bf16[112,1024]{1,0:T(8,128)(2,1)S(1)}, bf16[112,1024]{1,0:T(8,128)(2,1)S(1)}, u32[]{:S(2)}, u32[]{:S(2)}) collective-permute-start(bf16[112,1024]{1,0:T(8,128)(2,1)S(1)} %slice.7), channel_id=1, source_target_pairs={{0,8},{8,16},{16,24},{24,0},{32,40},{40,48},{48,56},{56,32},{64,72... | collective-permute-start | bytes 688136 | tf_op jit(solution)/shard_map/ppermute | solution.py:378
  46.5 8.7 %collective-permute-start.2 = (bf16[112,1024]{1,0:T(8,128)(2,1)S(1)}, bf16[112,1024]{1,0:T(8,128)(2,1)S(1)}, u32[]{:S(2)}, u32[]{:S(2)}) collective-permute-start(bf16[112,1024]{1,0:T(8,128)(2,1)S(1)} %slice.6), channel_id=1, source_target_pairs={{0,24},{8,0},{16,8},{24,16},{32,56},{40,32},{48,40},{56,48},{64,88... | collective-permute-start | bytes 688136 | tf_op jit(solution)/shard_map/ppermute | solution.py:377
  88.3 15.4 %copy-start = (bf16[1024,1024]{1,0:T(8,128)(2,1)S(1)}, bf16[1024,1024]{1,0:T(8,128)(2,1)}, u32[]{:S(2)}) copy-start(bf16[1024,1024]{1,0:T(8,128)(2,1)} %weight_ref.1) | copy-start | bytes 6291460
  90.4 21.4 %all-to-all-start.4 = ((bf16[8,32,1024]{2,1,0:T(8,128)(2,1)}), bf16[8,32,1024]{2,1,0:T(8,128)(2,1)S(1)}, u32[]{:S(2)}, u32[]{:S(2)}) async-start(bf16[8,32,1024]{2,1,0:T(8,128)(2,1)} %bitcast.6), calls=%async_computation.4 | async-start | bytes 1048576 | tf_op jit(solution)/shard_map/all_to_all | solution.py:388
  93.9 1.4 %collective-permute-start.4 = (bf16[224,128]{1,0:T(8,128)(2,1)S(1)}, bf16[224,128]{1,0:T(8,128)(2,1)S(1)}, u32[]{:S(2)}, u32[]{:S(2)}) collective-permute-start(bf16[224,128]{1,0:T(8,128)(2,1)S(1)} %get-tuple-element.46), channel_id=1, source_target_pairs={{0,1},{1,0},{2,3},{3,2},{4,5},{5,4},{6,7},{7,6},{8,9},{9,8},{10,11... | collective-permute-start | bytes 172040 | tf_op jit(solution)/shard_map/ppermute | solution.py:389
  95.3 5.7 %collective-permute-start.7 = (bf16[2,224,128]{2,1,0:T(8,128)(2,1)S(1)}, bf16[2,224,128]{2,1,0:T(8,128)(2,1)S(1)}, u32[]{:S(2)}, u32[]{:S(2)}) collective-permute-start(bf16[2,224,128]{2,1,0:T(8,128)(2,1)S(1)} %pad_maximum_fusion.pair_0), channel_id=1, source_target_pairs={{6,0},{7,1},{0,2},{1,3},{2,4},{3,5},{4,6},{5,7},{14,8},{15,9},{8,1... | collective-permute-start | bytes 344072 | tf_op jit(solution)/shard_map/ppermute | solution.py:394
  95.9 7.6 %collective-permute-start.6 = (bf16[2,224,128]{2,1,0:T(8,128)(2,1)S(1)}, bf16[2,224,128]{2,1,0:T(8,128)(2,1)S(1)}, u32[]{:S(2)}, u32[]{:S(2)}) collective-permute-start(bf16[2,224,128]{2,1,0:T(8,128)(2,1)S(1)} %pad_maximum_fusion.pair_0), channel_id=1, source_target_pairs={{4,0},{5,1},{6,2},{7,3},{0,4},{1,5},{2,6},{3,7},{12,8},{13,9},{14,... | collective-permute-start | bytes 344072 | tf_op jit(solution)/shard_map/ppermute | solution.py:394
  97.8 5.9 %collective-permute-start.5 = (bf16[2,224,128]{2,1,0:T(8,128)(2,1)S(1)}, bf16[2,224,128]{2,1,0:T(8,128)(2,1)S(1)}, u32[]{:S(2)}, u32[]{:S(2)}) collective-permute-start(bf16[2,224,128]{2,1,0:T(8,128)(2,1)S(1)} %pad_maximum_fusion.pair_0), channel_id=1, source_target_pairs={{2,0},{3,1},{4,2},{5,3},{6,4},{7,5},{0,6},{1,7},{10,8},{11,9},{12,... | collective-permute-start | bytes 344072 | tf_op jit(solution)/shard_map/ppermute | solution.py:394
